TPU v7x, 32 devices: a whole 2x2x4 slice. The times are simulated.
32 devices in a mesh: wide: 8 (over y, x, core), narrow: 4 (over z).
Axes of the slice: x: 2, y: 2, z: 4, core: 2. Of those that a mesh axis runs over, the one named last changes fastest.
Arguments:
- hidden: bfloat16 [4096, 14336], P('narrow', 'wide'), may hold values from -6 to 6
- out_grad: bfloat16 [4096, 4096], P('wide', 'narrow'), may hold values from -6 to 6
- sign_bits: int32 [14336, 4096], P('wide', 'narrow'), may hold values 0 or 1
- pick_rows: int32 [8192], replicated, may hold values from 0 to 14335
- pick_cols: int32 [8192], replicated, may hold values from 0 to 4095
Outputs:
- sketch: float32 [2, 8192], replicated
All inputs are finite; a program needn't handle non-finite values. No bound on the sum of `sign_bits` on one device may be relied on, other than what follows from the above.
Results may differ from a plain program's by a relative error of at most 0.0003.
Values may be sent and summed in bfloat16 or wider, within the bound.
No kernel may reach another device: no remote copies, remote signals or barrier semaphores. Data moves between devices by JAX's collectives and lax.ppermute only.
A program may use at most 128 MiB of HBM per device.

v0:
```python
import math

import jax
import jax.numpy as jnp
from jax import lax
from jax.sharding import PartitionSpec as P

EXAMPLES = 2
SEQ = 2048
GROUPS = 16
BAND = 128


def bit_parity(value, count):
    total = jnp.zeros_like(value)
    for bit_num in range(count):
        total = total + jnp.bitwise_and(jnp.right_shift(value, bit_num), 1)
    return total % 2


def walsh_table(length):
    numbers = lax.iota(jnp.int32, length)
    parity = bit_parity(
        jnp.bitwise_and(numbers[:, None], numbers[None, :]), length.bit_length() - 1
    )
    return (1 - 2 * parity).astype(jnp.float32) / math.sqrt(length)


def shards(hidden, out_grad, sign_bits, pick_rows, pick_cols):
    acts_all = lax.all_gather(hidden, "narrow", axis=0, tiled=True)
    grads_all = lax.all_gather(out_grad, "wide", axis=0, tiled=True)
    rows_local = acts_all.shape[1]
    cols_local = grads_all.shape[1]
    acts_all = acts_all.reshape(EXAMPLES, -1, rows_local)
    grads_all = grads_all.reshape(EXAMPLES, -1, cols_local)
    gradient = jnp.einsum("esr,esc->erc", acts_all, grads_all, preferred_element_type=jnp.float32)
    flipped = gradient * (2 * sign_bits - 1).astype(jnp.float32)[None]
    wide_count = lax.axis_size("wide")
    narrow_count = lax.axis_size("narrow")
    groups_local = GROUPS // wide_count
    middle = rows_local // (groups_local * BAND)
    blocks = flipped.reshape(EXAMPLES, groups_local, middle, BAND, cols_local)
    blocks = jnp.einsum(
        "ehmpc,gh->egmpc", blocks, walsh_table(groups_local), precision=lax.Precision.HIGHEST
    )
    blocks = jnp.einsum(
        "ehmpc,qp->ehmqc", blocks, walsh_table(BAND), precision=lax.Precision.HIGHEST
    )
    blocks = jnp.dot(
        blocks.reshape(-1, cols_local), walsh_table(cols_local), precision=lax.Precision.HIGHEST
    )
    local = blocks.reshape(EXAMPLES, rows_local * cols_local)
    position = pick_rows % rows_local * cols_local + pick_cols % cols_local
    row_owner = pick_rows // rows_local
    col_owner = pick_cols // cols_local
    wide_index = lax.axis_index("wide")
    narrow_index = lax.axis_index("narrow")
    picked = local[:, position]
    parity = bit_parity(
        jnp.bitwise_and(row_owner, wide_index), wide_count.bit_length() - 1
    ) + bit_parity(jnp.bitwise_and(col_owner, narrow_index), narrow_count.bit_length() - 1)
    weights = (1 - 2 * (parity % 2)).astype(jnp.float32) / math.sqrt(wide_count * narrow_count)
    terms = picked * weights[None, :]
    terms = terms * (1.0 / math.sqrt(SEQ))
    return lax.psum(terms, ("wide", "narrow"))


def solution(mesh):
    placed = (P("narrow", "wide"), P("wide", "narrow"), P("wide", "narrow"), P(), P())
    return jax.shard_map(shards, mesh=mesh, in_specs=placed, out_specs=P(), check_vma=False)
```

profile of v0, /device:TPU:0, one launch (start us, length us, event | category | flops | bytes accessed | tf_op | source)
XLA Modules:
  0.0 726.3 jit_solution(8760664690386254123)
XLA Ops:
  6.5 0.0 copy-start.1
  6.5 0.0 copy-start.2
  6.5 0.0 all-gather.5.cloned.1.call-start
  6.5 0.7 all-gather.5.cloned.1.call-update
  7.3 0.0 all-gather.3.cloned.1.call-start
  7.3 0.7 all-gather.3.cloned.1.call-update
  8.0 0.0 all-reduce.2.cloned.1.call-start
  8.1 0.0 copy-done.1
  8.1 0.0 copy-done.2
  8.1 0.1 fusion.47
  8.3 7.8 %add_convert_fusion = f32[1792,1024]{1,0:T(8,128)} fusion(s32[1792,1024]{1,0:T(8,128)} %param.7), kind=kLoop, calls=%fused_computation.7 | loop fusion | flops 5505024 | bytes 14680064 | tf_op jit(solution)/shard_map/convert_element_type | solution.py:37
  16.0 7.0 fusion.108
  23.1 43.3 %all-gather.5.cloned.1.call-done = bf16[4096,1024]{1,0:T(8,128)(2,1)} async-done(((bf16[512,1024]{1,0:T(8,128)(2,1)}), bf16[4096,1024]{1,0:T(8,128)(2,1)}) %all-gather.5.cloned.1.call-update) | async-done | bytes 8388624 | tf_op jit(solution)/shard_map/all_gather | solution.py:31
  66.4 254.1 %all-gather.3.cloned.1.call-done = bf16[4096,1792]{1,0:T(8,128)(2,1)} async-done(((bf16[1024,1792]{1,0:T(8,128)(2,1)}), bf16[4096,1792]{1,0:T(8,128)(2,1)}) %all-gather.3.cloned.1.call-update) | async-done | bytes 14680080 | tf_op jit(solution)/shard_map/all_gather | solution.py:30
  320.5 24.7 %convolution_multiply_fusion = f32[2,1792,1024]{2,1,0:T(8,128)} fusion(bf16[2,2048,1792]{2,1,0:T(8,128)(2,1)} %bitcast.30, bf16[2,2048,1024]{2,1,0:T(8,128)(2,1)} %bitcast.31, f32[1792,1024]{1,0:T(8,128)} %add_convert_fusion), kind=kOutput, calls=%fused_computation.6 | convolution fusion | flops 15036055552 | bytes 45088768 | tf_op jit(solution)/shard_map/esr,esc->erc/dot_general | solution.py:36
  345.2 69.9 %fusion.3 = f32[2,2,7,128,1024]{4,0,3,2,1:T(2,128)S(1)} fusion(f32[2,2,7,128,1024]{4,3,2,1,0:T(8,128)} %bitcast.28), kind=kOutput, calls=%fused_computation.4 | convolution fusion | flops 88080456 | bytes 29360128 | tf_op jit(solution)/shard_map/ehmpc,gh->egmpc/dot_general | solution.py:43
  415.1 0.0 copy-start
  415.1 18.5 %fusion = f32[128,2,2,7,1024]{4,0,3,2,1:T(8,128)} fusion(f32[2,2,7,128,1024]{4,0,3,2,1:T(2,128)S(1)} %fusion.3), kind=kOutput, calls=%fused_computation.1 | convolution fusion | flops 5637734400 | bytes 29360128 | tf_op jit(solution)/shard_map/ehmpc,qp->ehmqc/dot_general | solution.py:46
  433.6 0.0 copy-done
  433.6 51.5 %fusion.10 = f32[3584,1024]{1,0:T(8,128)} fusion(f32[3584,1024]{1,0:T(8,128)} %bitcast.29, f32[1024,1024]{1,0:T(8,128)S(1)} %copy-done), kind=kOutput, calls=%fused_computation.16 | convolution fusion | flops 45097156608 | bytes 33554432 | tf_op jit(solution)/shard_map/dot_general | solution.py:49
  485.2 24.8 %reshape.21 = f32[2,1835008]{1,0:T(2,128)} reshape(f32[3584,1024]{1,0:T(8,128)} %fusion.10) | data formatting | bytes 29360128 | tf_op jit(solution)/shard_map/reshape | solution.py:52
  510.0 91.3 %gather_fusion = f32[8192,2]{0,1:T(2,128)S(1)} fusion(f32[2,1835008]{1,0:T(2,128)} %reshape.21, s32[8192]{0:T(1024)S(1)} %fusion.48), kind=kCustom, calls=%fused_computation | custom fusion | bytes 163840 | tf_op jit(solution)/shard_map/gather | solution.py:58
  601.3 0.7 multiply_bitcast_fusion
  602.0 0.0 all-reduce.2.cloned.1.call-update
  602.0 115.8 %all-reduce.2.cloned.1.call-done = f32[2,8192]{1,0:T(2,128)} async-done(((f32[2,8192]{1,0:T(2,128)}), f32[2,8192]{1,0:T(2,128)}) %all-reduce.2.cloned.1.call-update) | async-done | bytes 65552 | tf_op jit(solution)/shard_map/psum | solution.py:65
  717.9 1.5 copy.20
  (1 shorter events, 0.0 us)
Async XLA Ops:
  6.5 1.5 copy-start.1
  6.5 1.5 copy-start.2
  6.5 59.8 %all-gather.5.cloned.1.call-start = ((), (), s32[]{:S(2)}) async-start(), calls=%async_computation.1 | async-start | bytes 9437184 | tf_op jit(solution)/shard_map/all_gather | solution.py:31
  7.3 313.2 %all-gather.3.cloned.1.call-start = ((), (), s32[]{:S(2)}) async-start(), calls=%async_computation | async-start | bytes 18350080 | tf_op jit(solution)/shard_map/all_gather | solution.py:30
  8.0 709.9 %all-reduce.2.cloned.1.call-start = ((), (), s32[]{:S(2)}) async-start(), calls=%async_computation.2 | async-start | bytes 131072 | tf_op jit(solution)/shard_map/psum | solution.py:65
  415.1 18.6 %copy-start = (f32[1024,1024]{1,0:T(8,128)S(1)}, f32[1024,1024]{1,0:T(8,128)}, u32[]{:S(2)}) copy-start(f32[1024,1024]{1,0:T(8,128)} %fusion.108) | copy-start | bytes 12582916
Sparse Core Ops, SparseCore 0:
  9.2 57.0 all-gather.4
  67.9 252.4 all-gather.2
  602.2 115.6 all-reduce.1
where the time goes:
time: 735 us; the launch traced here: 726 us
  waiting for transfers between devices  415 us (56%)
  matrix products  165 us (22%)
  local copies, waits for them, and re-layouts  118 us (16%)
  other arithmetic  15.7 us (2%)
  between operations  13.6 us (2%)
    all_gather x1, waiting for transfers between devices, shards(): acts_all = lax.all_gather(hidden, 'narrow', axis=0, tiled=True)  254 us
    psum x1, waiting for transfers between devices, shards(): return lax.psum(terms, ('wide', 'narrow'))  116 us
    gather x1, local copies, waits for them, and re-layouts, shards(): picked = local[:, position]  91.3 us
    dot_general x1, matrix products, shards(): jnp.einsum('ehmpc,gh->egmpc', blocks, walsh_table(groups_local), precisio...  69.9 us
    dot_general x1, matrix products, shards(): jnp.dot(blocks.reshape(-1, cols_local), walsh_table(cols_local), precisio...  51.5 us
    all_gather x1, waiting for transfers between devices, shards(): grads_all = lax.all_gather(out_grad, 'wide', axis=0, tiled=True)  43.3 us
    reshape x1, local copies, waits for them, and re-layouts, shards(): local = blocks.reshape(EXAMPLES, rows_local * cols_local)  24.8 us
    dot_general x1, matrix products, shards(): jnp.einsum('esr,esc->erc', acts_all, grads_all, preferred_element_type=jn...  24.7 us
  transfers between devices with their start and end apart: 3, of which 3 were waited for; matrix products, arithmetic and copies ran while one was open for 2% of the time, Pallas kernels for 0%

commit v1 on v0

v1 whole, which is shorter than its diff:
```python
import functools
import math

import jax
import jax.numpy as jnp
from jax import lax
from jax.experimental import pallas as pl
from jax.experimental.pallas import tpu as pltpu
from jax.sharding import PartitionSpec as P

EXAMPLES = 2
SEQ = 2048
GROUPS = 16
BAND = 128
LANES = 128


def bit_parity(value, count):
    total = jnp.zeros_like(value)
    for bit_num in range(count):
        total = total + jnp.bitwise_and(jnp.right_shift(value, bit_num), 1)
    return total % 2


def two_parts(value):
    high = value.astype(jnp.bfloat16)
    low = (value - high.astype(jnp.float32)).astype(jnp.bfloat16)
    return high, low


def dot(left, right):
    return jnp.dot(left, right, preferred_element_type=jnp.float32)


def piece_kernel(blocks, groups, grad_counts, scalars, *refs):
    refs = list(refs)
    take = lambda count: [refs.pop(0) for _ in range(count)]
    parts, found, *sample_scratch, arrived = refs[-7:]
    sides = len(grad_counts)
    acts = [take(groups) for _ in range(blocks)]
    grads = [take(count) for count in grad_counts]
    signs = [take(groups) for _ in range(sides)]
    sample_refs = take(4)
    (out,) = take(1)
    row_signs, col_signs, spots, lines = sample_scratch
    rows = groups * BAND
    cols = parts.shape[0] // sides
    picks = row_signs.shape[1]
    span_cols = min(4 * LANES, picks)
    step = pl.program_id(0)
    copies = [
        pltpu.make_async_copy(source, target, arrived.at[number])
        for number, (source, target) in enumerate(zip(sample_refs, sample_scratch))
    ]

    @pl.when((step == 0) & (scalars[0] != 0))
    def _():
        for copy in copies:
            copy.start()

    @pl.when(step == 0)
    def _():
        out[...] = jnp.zeros_like(out)

    @pl.when(scalars[0] != 0)
    def _():
        for side in range(sides):
            left = jnp.concatenate([ref[...] for ref in grads[side]], axis=1)
            right = [jnp.concatenate([ref[...] for ref in block], axis=1) for block in acts]
            total = dot(left, jnp.concatenate(right, axis=0))
            flips = []
            for ref in signs[side]:
                flip = ref[...].astype(jnp.float32)
                flips.append((2 * flip - 1 if ref.dtype == jnp.int32 else flip).T)
            high, low = two_parts(total * jnp.concatenate(flips, axis=1))
            parts[side * cols : (side + 1) * cols, :rows] = high
            parts[side * cols : (side + 1) * cols, rows:] = low

    @pl.when((step == 0) & (scalars[0] != 0))
    def _():
        for copy in copies:
            copy.wait()

    @pl.when(scalars[0] != 0)
    def _():
        begin = scalars[1 + step]
        end = scalars[2 + step]

        def sample(at, carry):
            first = pl.multiple_of(at * span_cols, span_cols)
            span = pl.ds(first, span_cols)
            right = jnp.concatenate([row_signs[:, span]] * 2, axis=0)

            def sign_of(bit):
                return col_signs[pl.ds(8 + bit - 3, 1), span]

            def join(levels, value, place, bit):
                while place & 1:
                    value = levels.pop() + sign_of(bit) * value
                    place, bit = place >> 1, bit + 1
                levels.append(value)

            outer = []
            for side in range(sides):
                values = dot(parts[side * cols : (side + 1) * cols, :], right)
                for place in range(cols // 8):
                    join(outer, values[place * 8 : place * 8 + 8], side * cols // 8 + place, 3)
            (value,) = outer
            value = jnp.sum(value * col_signs[:8, span], axis=0, keepdims=True)
            places = first + lax.broadcasted_iota(jnp.int32, (1, span_cols), 1)
            inside = (places >= begin) & (places < end)
            found[:, span] = jnp.where(inside, value, found[:, span])
            return carry

        lax.fori_loop(begin // span_cols, (end + span_cols - 1) // span_cols, sample, 0)

        @pl.when(step == pl.num_programs(0) - 1)
        def _():
            start = scalars[1]
            wide_cols = min(8 * LANES, picks)

            def spread(at, carry):
                first = pl.multiple_of(at * wide_cols, wide_cols)
                span = pl.ds(first, wide_cols)
                places = first + lax.broadcasted_iota(jnp.int32, (1, wide_cols), 1)
                inside = (places >= start) & (places < end)
                value = jnp.where(inside, found[:, span], 0.0)
                value = lines[:, span].astype(jnp.float32) * value
                high, low = two_parts(value)
                out[...] += dot(high, spots[span, :]) + dot(low, spots[span, :])
                return carry

            lax.fori_loop(start // wide_cols, (end + wide_cols - 1) // wide_cols, spread, 0)


def piece(steps, groups, scalars, acts, grads, signs, samples):
    sides = len(signs)
    cols = signs[0][0].shape[1]
    rows = groups * BAND
    picks = samples[0].shape[1]
    operands, specs = [], []

    def column_map(row_block, middle, first, group, step, scalars):
        return row_block, group * middle + first + step * scalars[0]

    for array, depth, row_block, middle, first in acts:
        for group in range(groups):
            operands.append(array)
            specs.append(
                pl.BlockSpec(
                    (depth, BAND), functools.partial(column_map, row_block, middle, first, group)
                )
            )

    def fixed_map(row_block, step, scalars):
        if isinstance(row_block, tuple):
            row_block = scalars[row_block[0]] + row_block[1]
        return row_block, 0

    once = pl.Buffered(1)
    for per_side in grads:
        for array, depth, row_block in per_side:
            operands.append(array)
            specs.append(
                pl.BlockSpec(
                    (cols, depth), functools.partial(fixed_map, row_block), pipeline_mode=once
                )
            )

    def row_map(middle, first, group, step, scalars):
        return group * middle + first + step * scalars[0], 0

    for array, middle, first in signs:
        for group in range(groups):
            operands.append(array)
            specs.append(
                pl.BlockSpec((BAND, cols), functools.partial(row_map, middle, first, group))
            )
    for array in samples:
        operands.append(array)
        specs.append(pl.BlockSpec(memory_space=pl.ANY))
    depth = sum(act[1] for act in acts)
    work = rows * cols * sides
    return pl.pallas_call(
        functools.partial(piece_kernel, len(acts), groups, [len(each) for each in grads]),
        grid_spec=pltpu.PrefetchScalarGridSpec(
            num_scalar_prefetch=1,
            grid=(steps,),
            in_specs=specs,
            out_specs=pl.BlockSpec((picks // LANES, LANES), functools.partial(fixed_map, 0)),
            scratch_shapes=[
                pltpu.VMEM((sides * cols, 2 * rows), jnp.bfloat16),
                pltpu.VMEM((1, picks), jnp.float32),
                *[pltpu.VMEM(array.shape, array.dtype) for array in samples],
                pltpu.SemaphoreType.DMA((len(samples),)),
            ],
        ),
        out_shape=jax.ShapeDtypeStruct((picks // LANES, LANES), jnp.float32),
        compiler_params=pltpu.CompilerParams(vmem_limit_bytes=48 * 1024 * 1024),
        cost_estimate=pl.CostEstimate(flops=1, bytes_accessed=1, transcendentals=0),
    )(scalars, *operands)


def after(value, *earlier):
    return lax.optimization_barrier((value, *earlier))[0]


def middle_slice(array, axis, groups, middle, first, count):
    cuts = []
    for group in range(groups):
        start = (group * middle + first) * BAND
        cuts.append(lax.slice_in_dim(array, start, start + count * BAND, axis=axis))
    return jnp.concatenate(cuts, axis=axis)


def sum_over(value, axis):
    size = lax.axis_size(axis)
    stride = 1
    while stride < size:
        pairs = [(index, index ^ stride) for index in range(size)]
        value = value + lax.ppermute(value, axis, pairs)
        stride = stride * 2
    return value


def ordered_samples(pick_rows, pick_cols, rows_local, cols_local, groups, middle):
    picks = pick_rows.shape[0]
    rows = groups * BAND
    row_here = pick_rows % rows_local
    pick_middle = row_here // BAND % middle
    row_place = row_here // (middle * BAND) * BAND + row_here % BAND
    col_place = pick_cols % (2 * cols_local)
    numbers = lax.iota(jnp.int32, picks)
    key, payload = lax.sort(
        (pick_middle * picks + numbers, row_place * (2 * cols_local) + col_place), num_keys=1
    )
    numbers = key % picks
    col_place = payload % (2 * cols_local)
    row_place = payload // (2 * cols_local)
    heads = lax.iota(jnp.int32, middle + 1)
    starts = jnp.sum((pick_middle[None, :] < heads[:, None]).astype(jnp.int32), axis=1)

    def signs(counted, kind):
        return (1 - 2 * (lax.population_count(counted) & 1)).astype(kind)

    row_signs = signs(row_place[None, :] & lax.iota(jnp.int32, rows)[:, None], jnp.bfloat16)
    bits = (2 * cols_local).bit_length() - 1
    masks = list(range(8)) + [1 << bit for bit in range(3, bits)]
    masks = jnp.array(masks + [0] * (-len(masks) % 8), jnp.int32)
    col_signs = signs(col_place[None, :] & masks[:, None], jnp.float32)
    lanes = lax.iota(jnp.int32, LANES)
    spots = (numbers[:, None] % LANES == lanes[None, :]).astype(jnp.bfloat16)
    lines = lax.iota(jnp.int32, picks // LANES)
    lines = (numbers[None, :] // LANES == lines[:, None]).astype(jnp.bfloat16)
    return (row_signs, col_signs, spots, lines), starts


def shards(hidden, out_grad, sign_bits, pick_rows, pick_cols):
    wide_count = lax.axis_size("wide")
    narrow_count = lax.axis_size("narrow")
    wide_index = lax.axis_index("wide")
    narrow_index = lax.axis_index("narrow")
    rows_local = hidden.shape[1]
    cols_local = out_grad.shape[1]
    tokens_local = hidden.shape[0]
    picks = pick_rows.shape[0]
    groups = GROUPS // wide_count
    rows = groups * BAND
    middle = rows_local // rows
    half = wide_count // EXAMPLES
    line = narrow_count == 4 and tokens_local * 2 == SEQ and half * 2 == wide_count

    samples, starts = ordered_samples(
        pick_rows, pick_cols, rows_local, cols_local, groups, middle
    )

    def scalars(active, first, count, *indices):
        parts = [jnp.int32(active)[None], starts[first : first + count + 1]]
        return jnp.concatenate(parts + [index[None] for index in indices])

    if line:
        partner = [(0, 1), (1, 0), (2, 3), (3, 2)]
        inner = [(1, 2), (2, 1)]
        inward = [(0, 1), (3, 2)]
        outward = [(1, 0), (2, 3)]
        split = middle // 2
        near = narrow_index // 2
        is_inner = ((narrow_index == 1) | (narrow_index == 2)).astype(jnp.int32)

        all_grads = lax.all_gather(out_grad.T, "wide", axis=0, tiled=True)
        tokens = out_grad.shape[0]
        depth = out_grad.shape[0] // 2
        swaps = [[], []]
        for z in range(4):
            for w in range(half):
                source = (half * (1 - z // 2) + w) * 4 + z
                for part in range(2):
                    swaps[part].append((source, (2 * w + part) * 4 + z))
        first_part = lax.ppermute(out_grad[:depth], ("wide", "narrow"), swaps[0])
        second_part = lax.ppermute(out_grad[depth:], ("wide", "narrow"), swaps[1])
        share = jnp.where(wide_index % 2 == 0, first_part, second_part).T

        def far_signs(first, count):
            cut = middle_slice(sign_bits, 0, groups, middle, first, count)
            return (2 * cut - 1).astype(jnp.bfloat16)

        def send(value, pairs, *earlier):
            return lax.ppermute(after(value, *earlier), "narrow", pairs)

        mid = send(hidden, inner)
        paired = send(hidden, partner)
        share = send(share, inward)
        shared = lax.all_gather(share, "wide", axis=0, tiled=True)

        def paired_part(first, count):
            return middle_slice(paired, 1, groups, middle, first, count)

        second = send(paired_part(0, split), inner)
        far_cuts = [(split, middle - 2 - split), (middle - 2, 1), (middle - 1, 1)]
        seconds = [send(paired_part(*cut), inner) for cut in far_cuts]
        flips = send(far_signs(split, middle - split), inward, paired)

        shared_tokens = share.shape[1]

        def token_blocks(array, indices):
            tokens = array.shape[1]
            return [
                (array, tokens, (index, part))
                for index in indices
                for part in range(tokens_local // tokens)
            ]

        def first_of(tokens, block):
            return block * (tokens_local // tokens)

        near_sum = piece(
            middle,
            groups,
            scalars(
                1,
                0,
                middle,
                first_of(tokens, narrow_index),
                first_of(tokens, narrow_index ^ 1),
            ),
            [(hidden, tokens_local, 0, middle, 0), (paired, tokens_local, 0, middle, 0)],
            [token_blocks(all_grads, (middle + 2, middle + 3))],
            [(sign_bits, middle, 0)],
            samples,
        )

        far_one = 2 - near
        far_two = far_one ^ 1

        far_at = [
            first_of(tokens, far_one),
            first_of(tokens, far_two),
            first_of(shared_tokens, far_one % 2),
            first_of(shared_tokens, far_two % 2),
        ]

        def own_far_piece(active, one, two):
            return piece(
                split,
                groups,
                scalars(active, 0, split, *far_at[:2]),
                [
                    (one, tokens_local, 0, one.shape[1] // rows, 0),
                    (two, tokens_local, 0, split, 0),
                ],
                [token_blocks(all_grads, (split + 2, split + 3))],
                [(sign_bits, middle, 0)],
                samples,
            )

        def far_piece(first, count, received, flips):
            at = count + 2
            return piece(
                count,
                groups,
                scalars(is_inner, first, count, *far_at),
                [
                    (mid, tokens_local, 0, middle, first),
                    (received, tokens_local, 0, count, 0),
                ],
                [
                    token_blocks(all_grads, (at, at + 1)),
                    token_blocks(shared, (at + 2, at + 3)),
                ],
                [(sign_bits, middle, first), (flips, middle - split, first - split)],
                samples,
            )

        second = after(second, near_sum)
        end_one = send(middle_slice(mid, 1, groups, middle, 0, split), outward, near_sum)
        end_two = send(second, outward)
        far_sums = [own_far_piece(is_inner, mid, second)]
        for index, cut in enumerate(far_cuts):
            done = far_sums[-1]
            if index == len(far_cuts) - 1:
                one, two = after(end_one, done), after(end_two, done)
                far_sums.append(own_far_piece(1 - is_inner, one, two))
                done = far_sums[-1]
            far_sums.append(far_piece(*cut, after(seconds[index], done), after(flips, done)))
        far_sum = functools.reduce(jnp.add, far_sums)
        sums = jnp.where(
            near == 0, jnp.stack([near_sum, far_sum]), jnp.stack([far_sum, near_sum])
        )
    else:
        acts_all = lax.all_gather(hidden, "narrow", axis=0, tiled=True)
        all_grads = lax.all_gather(out_grad.T, "wide", axis=0, tiled=True)
        tokens = out_grad.shape[0]
        sums = jnp.stack(
            [
                piece(
                    middle,
                    groups,
                    scalars(1, 0, middle),
                    [(acts_all, SEQ, example, middle, 0)],
                    [
                        [
                            (all_grads, tokens, example * (SEQ // tokens) + part)
                            for part in range(SEQ // tokens)
                        ]
                    ],
                    [(sign_bits, middle, 0)],
                    samples,
                )
                for example in range(EXAMPLES)
            ]
        )
    parity = bit_parity(
        jnp.bitwise_and(pick_rows // rows_local, wide_index), wide_count.bit_length() - 1
    ) + bit_parity(
        jnp.bitwise_and(pick_cols // cols_local, narrow_index), narrow_count.bit_length() - 1
    )
    scale = 1.0 / math.sqrt(GROUPS * BAND * cols_local * narrow_count * SEQ)
    weights = (1 - 2 * (parity % 2)).astype(jnp.float32) * scale
    terms = sums.reshape(EXAMPLES, picks) * weights[None]
    return sum_over(sum_over(terms, "wide"), "narrow")


def solution(mesh):
    placed = (P("narrow", "wide"), P("wide", "narrow"), P("wide", "narrow"), P(), P())
    return jax.shard_map(shards, mesh=mesh, in_specs=placed, out_specs=P(), check_vma=False)
```

time: 735 us -> 279 us (0.38); the launches traced: 726 us -> 279 us
  waiting for transfers between devices: 415 us -> 120 us
  matrix products: 165 us -> 0 us
  local copies, waits for them, and re-layouts: 118 us -> 16.8 us
  Pallas kernels: 0 us -> 69.1 us
  starting transfers between devices: 0.08 us -> 34.4 us
  other arithmetic: 15.7 us -> 24.9 us
    all_gather x2, waiting for transfers between devices: 297 us -> 0.02 us  [the longest x1 0.02 us: shards(): shared = lax.all_gather(share, 'wide', axis=0, tiled=True)]
    dot_general x4 -> x0, matrix products: 165 us -> none  [the longest x1 69.9 us: shards(): jnp.einsum('ehmpc,gh->egmpc', blocks, walsh_table(groups_local), precisio...]
    ppermute x0 -> x17, waiting for transfers between devices: none -> 119 us  [the longest x10 97.3 us: send(): return lax.ppermute(after(value, *earlier), 'narrow', pairs)]
    psum x1 -> x0, waiting for transfers between devices: 116 us -> none  [shards(): return lax.psum(terms, ('wide', 'narrow'))]
    gather x1 -> x0, local copies, waits for them, and re-layouts: 91.3 us -> none  [shards(): picked = local[:, position]]
    pallas_call x0 -> x6, Pallas kernels: none -> 69.1 us  [piece(): pl.pallas_call(functools.partial(piece_kernel, len(acts), groups, [len(ea...]
    ppermute x0 -> x17, starting transfers between devices: none -> 34.4 us  [the longest x10 29.1 us: send(): return lax.ppermute(after(value, *earlier), 'narrow', pairs)]
    reshape x1 -> x0, local copies, waits for them, and re-layouts: 24.8 us -> none  [shards(): local = blocks.reshape(EXAMPLES, rows_local * cols_local)]
  transfers between devices with their start and end apart: 3 -> 19, of which waited for: 3 -> 9; matrix products, arithmetic and copies ran while one was open for 2% -> 12% of each run, Pallas kernels for 0% -> 23%
where the time goes in v1:
time: 279 us
  waiting for transfers between devices  120 us (43%)
  Pallas kernels  69.1 us (25%)
  starting transfers between devices  34.4 us (12%)
  other arithmetic  24.9 us (9%)
  local copies, waits for them, and re-layouts  16.8 us (6%)
  between operations  13.8 us (5%)
    ppermute x10, waiting for transfers between devices, send(): return lax.ppermute(after(value, *earlier), 'narrow', pairs)  97.3 us
    pallas_call x6, Pallas kernels, piece(): pl.pallas_call(functools.partial(piece_kernel, len(acts), groups, [len(ea...  69.1 us
    ppermute x10, starting transfers between devices, send(): return lax.ppermute(after(value, *earlier), 'narrow', pairs)  29.1 us
    ppermute x5, waiting for transfers between devices, sum_over(): value = value + lax.ppermute(value, axis, pairs)  16.7 us
    slice x5, local copies, waits for them, and re-layouts, middle_slice(): cuts.append(lax.slice_in_dim(array, start, start + count * BAND, axis=axis))  8.94 us
    sort x1, other arithmetic, ordered_samples(): lax.sort((pick_middle * picks + numbers, row_place * (2 * cols_local) + c...  6.89 us
    unnamed x19, local copies, waits for them, and re-layouts  6.22 us
  transfers between devices with their start and end apart: 19, of which 9 were waited for; matrix products, arithmetic and copies ran while one was open for 12% of the time, Pallas kernels for 23%

profile of v1, /device:TPU:0, one launch (start us, length us, event | category | flops | bytes accessed | tf_op | source)
XLA Modules:
  0.0 278.6 jit_solution(3873949233746808654)
XLA Ops:
  6.5 2.3 copy.10
  8.9 3.1 %collective-permute-start = (bf16[1024,1792]{1,0:T(8,128)(2,1)}, bf16[1024,1792]{1,0:T(8,128)(2,1)}, u32[]{:S(2)}, u32[]{:S(2)}) collective-permute-start(bf16[1024,1792]{1,0:T(8,128)(2,1)} %refs_1_.1), channel_id=1, source_target_pairs={{0,1},{1,0},{2,3},{3,2},{4,5},{5,4},{6,7},{7,6},{8,9},{9,8},{10,11... | collective-permute-start | bytes 11010056 | tf_op jit(solution)/shard_map/ppermute | solution.py:308
  12.0 2.4 collective-permute-start.1
  17.9 6.9 %sort.23 = (s32[8192]{0:T(1024)S(1)}, s32[8192]{0:T(1024)S(1)}, s32[8192]{0:T(1024)}) sort(s32[8192]{0:T(1024)S(1)} %get-tuple-element.33, s32[8192]{0:T(1024)S(1)} %get-tuple-element.53, s32[8192]{0:T(1024)S(1)} %iota.23), dimensions={0}, to_apply=%region_1.2 | sort | flops 106496 | bytes 196608 | tf_op jit(solution)/shard_map/sort | solution.py:234
  24.8 3.9 %subtract_convert_fusion.refs_10_.refs_20_ = bf16[256,8192]{1,0:T(8,128)(2,1)} fusion(s32[8192]{0:T(1024)S(1)} %get-tuple-element.58), kind=kLoop, calls=%fused_computation | loop fusion | flops 12582912 | bytes 4227072 | tf_op jit(solution)/shard_map/convert_element_type | solution.py:244
  28.7 5.5 %collective-permute-done.4 = bf16[256,1024]{0,1:T(8,128)(2,1)S(1)} collective-permute-done((bf16[256,1024]{0,1:T(8,128)(2,1)S(1)}, bf16[256,1024]{0,1:T(8,128)(2,1)S(1)}, u32[]{:S(2)}, u32[]{:S(2)}) %collective-permute-start.4) | collective-permute-done | bytes 524320 | tf_op jit(solution)/shard_map/ppermute | solution.py:299
  34.3 7.0 %collective-permute-start.6 = (bf16[1024,256]{1,0:T(8,128)(2,1)S(1)}, bf16[1024,256]{1,0:T(8,128)(2,1)S(1)}, u32[]{:S(2)}, u32[]{:S(2)}) collective-permute-start(bf16[1024,256]{1,0:T(8,128)(2,1)S(1)} %select_bitcast_fusion), channel_id=1, source_target_pairs={{0,1},{3,2},{4,5},{7,6},{8,9},{11,10},{12,13},{15,14},{16,17},{19,... | collective-permute-start | bytes 1572872 | tf_op jit(solution)/shard_map/ppermute | solution.py:308
  41.3 2.8 fusion.30
  44.1 2.1 fusion.1
  46.1 55.9 %collective-permute-done.6 = bf16[1024,256]{1,0:T(8,128)(2,1)S(1)} collective-permute-done((bf16[1024,256]{1,0:T(8,128)(2,1)S(1)}, bf16[1024,256]{1,0:T(8,128)(2,1)S(1)}, u32[]{:S(2)}, u32[]{:S(2)}) %collective-permute-start.6) | collective-permute-done | bytes 524320 | tf_op jit(solution)/shard_map/ppermute | solution.py:308
  102.9 3.7 %fusion.2.refs_12_.refs_22_ = bf16[8192,128]{1,0:T(8,128)(2,1)S(1)} fusion(s32[8192]{0:T(1024)S(1)} %get-tuple-element.50), kind=kLoop, calls=%fused_computation.5 | loop fusion | flops 2097152 | bytes 2129920 | tf_op jit(solution)/shard_map/convert_element_type | solution.py:252
  106.8 2.1 fusion.31
  110.2 1.8 collective-permute-start.2
  112.0 7.4 %collective-permute-start.7 = (bf16[1024,1024]{1,0:T(8,128)(2,1)}, bf16[1024,1024]{1,0:T(8,128)(2,1)}, u32[]{:S(2)}, u32[]{:S(2)}) collective-permute-start(bf16[1024,1024]{1,0:T(8,128)(2,1)} %fusion.1), channel_id=1, source_target_pairs={{0,1},{3,2},{4,5},{7,6},{8,9},{11,10},{12,13},{15,14},{16,17},{19,... | collective-permute-start | bytes 6291464 | tf_op jit(solution)/shard_map/ppermute | solution.py:308
  120.6 1.5 fusion.34
  124.5 33.3 %shard_map.64 = f32[64,128]{1,0:T(8,128)S(1)} custom-call(s32[11]{0:T(128)S(1)} %pad_add_fusion.scalars, bf16[1024,1792]{1,0:T(8,128)(2,1)} %refs_1_.1, bf16[1024,1792]{1,0:T(8,128)(2,1)} %refs_1_.1, bf16[1024,1792]{1,0:T(8,128)(2,1)} %collective-permute-done.refs_2_.refs_3_, bf16[1024,1792]{1,0:T(8,128)(2,1)} %collective-permute-done.refs_2_.refs_3_, ...), custom_call_target="tpu_custom_call" | custom-call | flops 1 | bytes 1 | tf_op jit(solution)/shard_map/pallas_call | solution.py:184
  163.0 1.8 collective-permute-start.3
  167.0 1.5 collective-permute-start.8
  169.3 1.5 collective-permute-start.11
  172.2 3.5 %shard_map.65 = f32[64,128]{1,0:T(8,128)S(1)} custom-call(s32[7]{0:T(128)S(1)} %get-tuple-element.54.scalars, bf16[1024,1792]{1,0:T(8,128)(2,1)} %collective-permute-done.1.refs_0_.refs_1_, bf16[1024,1792]{1,0:T(8,128)(2,1)} %collective-permute-done.1.refs_0_.refs_1_, bf16[1024,768]{1,0:T(8,128)(2,1)} %collective-permute-done.2.refs_2_.refs_3_, ...), custom_call_target="tpu_custom_call" | custom-call | flops 1 | bytes 1 | tf_op jit(solution)/shard_map/pallas_call | solution.py:184
  176.8 5.1 %shard_map.66 = f32[64,128]{1,0:T(8,128)S(1)} custom-call(s32[8]{0:T(128)S(1)} %concatenate.41.scalars, bf16[1024,1792]{1,0:T(8,128)(2,1)} %collective-permute-done.1.refs_0_.refs_1_, bf16[1024,1792]{1,0:T(8,128)(2,1)} %collective-permute-done.1.refs_0_.refs_1_, bf16[1024,512]{1,0:T(8,128)(2,1)} %collective-permute-done.3.refs_2_.refs_3_, ...), custom_call_target="tpu_custom_call" | custom-call | flops 1 | bytes 1 | tf_op jit(solution)/shard_map/pallas_call | solution.py:184
  181.9 4.7 %shard_map.67 = f32[64,128]{1,0:T(8,128)S(1)} custom-call(s32[7]{0:T(128)S(1)} %concatenate.44.scalars, bf16[1024,1792]{1,0:T(8,128)(2,1)} %collective-permute-done.1.refs_0_.refs_1_, bf16[1024,1792]{1,0:T(8,128)(2,1)} %collective-permute-done.1.refs_0_.refs_1_, bf16[1024,256]{1,0:T(8,128)(2,1)} %collective-permute-done.8.refs_2_.refs_3_, ...), custom_call_target="tpu_custom_call" | custom-call | flops 1 | bytes 1 | tf_op jit(solution)/shard_map/pallas_call | solution.py:184
  186.7 10.7 %collective-permute-done.10.refs_2_.refs_3_ = bf16[1024,768]{1,0:T(8,128)(2,1)} collective-permute-done((bf16[1024,768]{1,0:T(8,128)(2,1)}, bf16[1024,768]{1,0:T(8,128)(2,1)}, u32[]{:S(2)}, u32[]{:S(2)}) %collective-permute-start.10) | collective-permute-done | bytes 1572896 | tf_op jit(solution)/shard_map/ppermute | solution.py:308
  197.4 30.6 %collective-permute-done.9.refs_0_.refs_1_ = bf16[1024,768]{1,0:T(8,128)(2,1)} collective-permute-done((bf16[1024,768]{1,0:T(8,128)(2,1)}, bf16[1024,768]{1,0:T(8,128)(2,1)}, u32[]{:S(2)}, u32[]{:S(2)}) %collective-permute-start.9) | collective-permute-done | bytes 1572896 | tf_op jit(solution)/shard_map/ppermute | solution.py:308
  228.0 17.8 %shard_map.68 = f32[64,128]{1,0:T(8,128)S(1)} custom-call(s32[7]{0:T(128)S(1)} %get-tuple-element.55.scalars, bf16[1024,768]{1,0:T(8,128)(2,1)} %collective-permute-done.9.refs_0_.refs_1_, bf16[1024,768]{1,0:T(8,128)(2,1)} %collective-permute-done.9.refs_0_.refs_1_, bf16[1024,768]{1,0:T(8,128)(2,1)} %collective-permute-done.10.refs_2_.refs_3_, ...), custom_call_target="tpu_custom_call" | custom-call | flops 1 | bytes 1 | tf_op jit(solution)/shard_map/pallas_call | solution.py:184
  245.8 4.7 %shard_map.69 = f32[64,128]{1,0:T(8,128)S(1)} custom-call(s32[7]{0:T(128)S(1)} %concatenate.48.scalars, bf16[1024,1792]{1,0:T(8,128)(2,1)} %collective-permute-done.1.refs_0_.refs_1_, bf16[1024,1792]{1,0:T(8,128)(2,1)} %collective-permute-done.1.refs_0_.refs_1_, bf16[1024,256]{1,0:T(8,128)(2,1)} %collective-permute-done.11.refs_2_.refs_3_, ...), custom_call_target="tpu_custom_call" | custom-call | flops 1 | bytes 1 | tf_op jit(solution)/shard_map/pallas_call | solution.py:184
  252.1 1.5 collective-permute-start.13
  253.7 2.8 collective-permute-done.13
  256.6 1.6 collective-permute-start.14
  258.2 2.7 collective-permute-done.14
  261.0 4.3 %collective-permute-done.15 = f32[2,8192]{1,0:T(2,128)S(1)} collective-permute-done((f32[2,8192]{1,0:T(2,128)S(1)}, f32[2,8192]{1,0:T(2,128)S(1)}, u32[]{:S(2)}, u32[]{:S(2)}) %collective-permute-start.15) | collective-permute-done | bytes 65568 | tf_op jit(solution)/shard_map/ppermute | solution.py:221
  265.4 5.7 %collective-permute-done.16 = f32[2,8192]{1,0:T(2,128)S(1)} collective-permute-done((f32[2,8192]{1,0:T(2,128)S(1)}, f32[2,8192]{1,0:T(2,128)S(1)}, u32[]{:S(2)}, u32[]{:S(2)}) %collective-permute-start.16) | collective-permute-done | bytes 65568 | tf_op jit(solution)/shard_map/ppermute | solution.py:221
  (70 shorter events, 22.6 us)
Async XLA Ops:
  6.5 11.2 %copy-start.7 = (s32[8192]{0:T(1024)S(1)}, s32[8192]{0:T(1024)}, u32[]{:S(2)}) copy-start(s32[8192]{0:T(1024)} %param.10) | copy-start | bytes 98308
  6.5 11.2 %copy-start.6 = (s32[8192]{0:T(1024)S(1)}, s32[8192]{0:T(1024)}, u32[]{:S(2)}) copy-start(s32[8192]{0:T(1024)} %param.9) | copy-start | bytes 98308
  6.5 116.9 %all-gather.3.cloned.1.call-start = ((), (), s32[]{:S(2)}) async-start(), calls=%async_computation | async-start | bytes 9437184 | tf_op jit(solution)/shard_map/all_gather | solution.py:290
  8.9 166.9 %all-gather.5.cloned.1.call-start = ((), (), s32[]{:S(2)}) async-start(), calls=%async_computation.1 | async-start | bytes 4718592 | tf_op jit(solution)/shard_map/all_gather | solution.py:313
  8.9 97.9 %collective-permute-start = (bf16[1024,1792]{1,0:T(8,128)(2,1)}, bf16[1024,1792]{1,0:T(8,128)(2,1)}, u32[]{:S(2)}, u32[]{:S(2)}) collective-permute-start(bf16[1024,1792]{1,0:T(8,128)(2,1)} %refs_1_.1), channel_id=1, source_target_pairs={{0,1},{1,0},{2,3},{3,2},{4,5},{5,4},{6,7},{7,6},{8,9},{9,8},{10,11... | collective-permute-start | bytes 11010056 | tf_op jit(solution)/shard_map/ppermute | solution.py:308
  12.0 108.6 %collective-permute-start.1 = (bf16[1024,1792]{1,0:T(8,128)(2,1)}, bf16[1024,1792]{1,0:T(8,128)(2,1)}, u32[]{:S(2)}, u32[]{:S(2)}) collective-permute-start(bf16[1024,1792]{1,0:T(8,128)(2,1)} %refs_1_.1), channel_id=1, source_target_pairs={{1,2},{2,1},{5,6},{6,5},{9,10},{10,9},{13,14},{14,13},{17,18},{18,... | collective-permute-start | bytes 11010056 | tf_op jit(solution)/shard_map/ppermute | solution.py:308
  15.7 18.5 %collective-permute-start.4 = (bf16[256,1024]{0,1:T(8,128)(2,1)S(1)}, bf16[256,1024]{0,1:T(8,128)(2,1)S(1)}, u32[]{:S(2)}, u32[]{:S(2)}) collective-permute-start(bf16[256,1024]{0,1:T(8,128)(2,1)S(1)} %get-tuple-element.48), channel_id=1, source_target_pairs={{16,0},{20,8},{24,16},{28,24},{17,1},{21,9},{25,17},{29,25},{2,2},... | collective-permute-start | bytes 1572872 | tf_op jit(solution)/shard_map/ppermute | solution.py:299
  17.0 17.2 %collective-permute-start.5 = (bf16[256,1024]{0,1:T(8,128)(2,1)S(1)}, bf16[256,1024]{0,1:T(8,128)(2,1)S(1)}, u32[]{:S(2)}, u32[]{:S(2)}) collective-permute-start(bf16[256,1024]{0,1:T(8,128)(2,1)S(1)} %get-tuple-element.47), channel_id=1, source_target_pairs={{16,4},{20,12},{24,20},{28,28},{17,5},{21,13},{25,21},{29,29},{2,6... | collective-permute-start | bytes 1572872 | tf_op jit(solution)/shard_map/ppermute | solution.py:300
  34.3 67.8 %collective-permute-start.6 = (bf16[1024,256]{1,0:T(8,128)(2,1)S(1)}, bf16[1024,256]{1,0:T(8,128)(2,1)S(1)}, u32[]{:S(2)}, u32[]{:S(2)}) collective-permute-start(bf16[1024,256]{1,0:T(8,128)(2,1)S(1)} %select_bitcast_fusion), channel_id=1, source_target_pairs={{0,1},{3,2},{4,5},{7,6},{8,9},{11,10},{12,13},{15,14},{16,17},{19,... | collective-permute-start | bytes 1572872 | tf_op jit(solution)/shard_map/ppermute | solution.py:308
  102.0 0.8 copy-start.5
  106.6 64.6 %copy-start = (bf16[8192,128]{1,0:T(8,128)(2,1)}, bf16[8192,128]{1,0:T(8,128)(2,1)S(1)}, u32[]{:S(2)}) copy-start(bf16[8192,128]{1,0:T(8,128)(2,1)S(1)} %fusion.2.refs_12_.refs_22_) | copy-start | bytes 6291460
  106.8 12.6 %copy-start.8 = (s32[16]{0:T(128)S(1)}, s32[16]{0:T(128)}, u32[]{:S(2)}) copy-start(s32[16]{0:T(128)} %constant.193.clone) | copy-start | bytes 196
  110.2 47.6 %collective-permute-start.2 = (bf16[1024,768]{1,0:T(8,128)(2,1)}, bf16[1024,768]{1,0:T(8,128)(2,1)}, u32[]{:S(2)}, u32[]{:S(2)}) collective-permute-start(bf16[1024,768]{1,0:T(8,128)(2,1)} %pad_maximum_fusion), channel_id=1, source_target_pairs={{1,2},{2,1},{5,6},{6,5},{9,10},{10,9},{13,14},{14,13},{17,18},{18,... | collective-permute-start | bytes 4718600 | tf_op jit(solution)/shard_map/ppermute | solution.py:308
  112.0 57.3 %collective-permute-start.7 = (bf16[1024,1024]{1,0:T(8,128)(2,1)}, bf16[1024,1024]{1,0:T(8,128)(2,1)}, u32[]{:S(2)}, u32[]{:S(2)}) collective-permute-start(bf16[1024,1024]{1,0:T(8,128)(2,1)} %fusion.1), channel_id=1, source_target_pairs={{0,1},{3,2},{4,5},{7,6},{8,9},{11,10},{12,13},{15,14},{16,17},{19,... | collective-permute-start | bytes 6291464 | tf_op jit(solution)/shard_map/ppermute | solution.py:308
  123.4 1.0 copy-start.1
  157.8 39.5 %collective-permute-start.10 = (bf16[1024,768]{1,0:T(8,128)(2,1)}, bf16[1024,768]{1,0:T(8,128)(2,1)}, u32[]{:S(2)}, u32[]{:S(2)}) collective-permute-start(bf16[1024,768]{1,0:T(8,128)(2,1)} %collective-permute-done.2.refs_2_.refs_3_), channel_id=1, source_target_pairs={{1,0},{2,3},{5,4},{6,7},{9,8},{10,11},{13,12},{14,15},{17,16},{18,... | collective-permute-start | bytes 4718600 | tf_op jit(solution)/shard_map/ppermute | solution.py:308
  159.1 68.9 %collective-permute-start.9 = (bf16[1024,768]{1,0:T(8,128)(2,1)}, bf16[1024,768]{1,0:T(8,128)(2,1)}, u32[]{:S(2)}, u32[]{:S(2)}) collective-permute-start(bf16[1024,768]{1,0:T(8,128)(2,1)} %pad_maximum_fusion.1), channel_id=1, source_target_pairs={{1,0},{2,3},{5,4},{6,7},{9,8},{10,11},{13,12},{14,15},{17,16},{18,... | collective-permute-start | bytes 4718600 | tf_op jit(solution)/shard_map/ppermute | solution.py:308
  163.0 12.7 %collective-permute-start.3 = (bf16[1024,512]{1,0:T(8,128)(2,1)}, bf16[1024,512]{1,0:T(8,128)(2,1)}, u32[]{:S(2)}, u32[]{:S(2)}) collective-permute-start(bf16[1024,512]{1,0:T(8,128)(2,1)} %pad_maximum_fusion.2), channel_id=1, source_target_pairs={{1,2},{2,1},{5,6},{6,5},{9,10},{10,9},{13,14},{14,13},{17,18},{18,... | collective-permute-start | bytes 3145736 | tf_op jit(solution)/shard_map/ppermute | solution.py:308
  167.0 14.9 %collective-permute-start.8 = (bf16[1024,256]{1,0:T(8,128)(2,1)}, bf16[1024,256]{1,0:T(8,128)(2,1)}, u32[]{:S(2)}, u32[]{:S(2)}) collective-permute-start(bf16[1024,256]{1,0:T(8,128)(2,1)} %pad_maximum_fusion.3), channel_id=1, source_target_pairs={{1,2},{2,1},{5,6},{6,5},{9,10},{10,9},{13,14},{14,13},{17,18},{18,... | collective-permute-start | bytes 1572872 | tf_op jit(solution)/shard_map/ppermute | solution.py:308
  169.3 76.5 %collective-permute-start.11 = (bf16[1024,256]{1,0:T(8,128)(2,1)}, bf16[1024,256]{1,0:T(8,128)(2,1)}, u32[]{:S(2)}, u32[]{:S(2)}) collective-permute-start(bf16[1024,256]{1,0:T(8,128)(2,1)} %pad_maximum_fusion.4), channel_id=1, source_target_pairs={{1,2},{2,1},{5,6},{6,5},{9,10},{10,9},{13,14},{14,13},{17,18},{18,... | collective-permute-start | bytes 1572872 | tf_op jit(solution)/shard_map/ppermute | solution.py:308
  171.2 1.0 copy-start.2
  175.8 1.0 copy-start.3
  181.9 46.1 %copy-start.4 = (f32[16,8192]{1,0:T(8,128)S(1)}, f32[16,8192]{1,0:T(8,128)}, u32[]{:S(2)}) copy-start(f32[16,8192]{1,0:T(8,128)} %subtract_convert_fusion.1.refs_11_.refs_21_) | copy-start | bytes 1572868
  250.7 1.3 collective-permute-start.12
  252.1 4.3 %collective-permute-start.13 = (f32[2,8192]{1,0:T(2,128)S(1)}, f32[2,8192]{1,0:T(2,128)S(1)}, u32[]{:S(2)}, u32[]{:S(2)}) collective-permute-start(f32[2,8192]{1,0:T(2,128)S(1)} %fusion.37), channel_id=1, source_target_pairs={{0,8},{4,12},{8,0},{12,4},{16,24},{20,28},{24,16},{28,20},{1,9},{5... | collective-permute-start | bytes 196616 | tf_op jit(solution)/shard_map/ppermute | solution.py:221
  256.6 4.3 %collective-permute-start.14 = (f32[2,8192]{1,0:T(2,128)S(1)}, f32[2,8192]{1,0:T(2,128)S(1)}, u32[]{:S(2)}, u32[]{:S(2)}) collective-permute-start(f32[2,8192]{1,0:T(2,128)S(1)} %fusion.38), channel_id=1, source_target_pairs={{0,16},{4,20},{8,24},{12,28},{16,0},{20,4},{24,8},{28,12},{1,17},{... | collective-permute-start | bytes 196616 | tf_op jit(solution)/shard_map/ppermute | solution.py:221
  261.0 4.3 %collective-permute-start.15 = (f32[2,8192]{1,0:T(2,128)S(1)}, f32[2,8192]{1,0:T(2,128)S(1)}, u32[]{:S(2)}, u32[]{:S(2)}) collective-permute-start(f32[2,8192]{1,0:T(2,128)S(1)} %add.138), channel_id=1, source_target_pairs={{0,1},{1,0},{2,3},{3,2},{4,5},{5,4},{6,7},{7,6},{8,9},{9,8},{10,11... | collective-permute-start | bytes 196616 | tf_op jit(solution)/shard_map/ppermute | solution.py:221
  265.3 5.8 %collective-permute-start.16 = (f32[2,8192]{1,0:T(2,128)S(1)}, f32[2,8192]{1,0:T(2,128)S(1)}, u32[]{:S(2)}, u32[]{:S(2)}) collective-permute-start(f32[2,8192]{1,0:T(2,128)S(1)} %add.139), channel_id=1, source_target_pairs={{0,2},{1,3},{2,0},{3,1},{4,6},{5,7},{6,4},{7,5},{8,10},{9,11},{10,... | collective-permute-start | bytes 196616 | tf_op jit(solution)/shard_map/ppermute | solution.py:221
Sparse Core Ops, SparseCore 0:
  9.2 66.2 all-gather.2
  103.0 37.8 all-gather.4

commit v2 on v1

--- a/solution.py
+++ b/solution.py
@@ -197,7 +197,9 @@
         ),
         out_shape=jax.ShapeDtypeStruct((picks // LANES, LANES), jnp.float32),
         compiler_params=pltpu.CompilerParams(vmem_limit_bytes=48 * 1024 * 1024),
-        cost_estimate=pl.CostEstimate(flops=1, bytes_accessed=1, transcendentals=0),
+        cost_estimate=pl.CostEstimate(
+            flops=8 * steps * work * depth, bytes_accessed=work, transcendentals=0
+        ),
     )(scalars, *operands)
 
 
@@ -282,8 +284,6 @@
         partner = [(0, 1), (1, 0), (2, 3), (3, 2)]
         inner = [(1, 2), (2, 1)]
         inward = [(0, 1), (3, 2)]
-        outward = [(1, 0), (2, 3)]
-        split = middle // 2
         near = narrow_index // 2
         is_inner = ((narrow_index == 1) | (narrow_index == 2)).astype(jnp.int32)
 
@@ -308,17 +308,17 @@
             return lax.ppermute(after(value, *earlier), "narrow", pairs)
 
         mid = send(hidden, inner)
-        paired = send(hidden, partner)
+        paired = after(send(hidden, partner), mid)
         share = send(share, inward)
         shared = lax.all_gather(share, "wide", axis=0, tiled=True)
 
         def paired_part(first, count):
             return middle_slice(paired, 1, groups, middle, first, count)
 
-        second = send(paired_part(0, split), inner)
-        far_cuts = [(split, middle - 2 - split), (middle - 2, 1), (middle - 1, 1)]
-        seconds = [send(paired_part(*cut), inner) for cut in far_cuts]
-        flips = send(far_signs(split, middle - split), inward, paired)
+        far_cuts = [(0, 2), (2, 2), (4, middle - 4)]
+        second_cuts = [(0, 4), far_cuts[2]]
+        seconds = [send(paired_part(*cut), inner) for cut in second_cuts]
+        flips = [send(far_signs(*cut), inward, paired) for cut in far_cuts]
 
         shared_tokens = share.shape[1]
 
@@ -359,21 +359,9 @@
             first_of(shared_tokens, far_two % 2),
         ]
 
-        def own_far_piece(active, one, two):
-            return piece(
-                split,
-                groups,
-                scalars(active, 0, split, *far_at[:2]),
-                [
-                    (one, tokens_local, 0, one.shape[1] // rows, 0),
-                    (two, tokens_local, 0, split, 0),
-                ],
-                [token_blocks(all_grads, (split + 2, split + 3))],
-                [(sign_bits, middle, 0)],
-                samples,
-            )
-
-        def far_piece(first, count, received, flips):
+        def far_piece(index, received, flips):
+            first, count = far_cuts[index]
+            second_first, second_count = second_cuts[index // 2]
             at = count + 2
             return piece(
                 count,
@@ -381,27 +369,22 @@
                 scalars(is_inner, first, count, *far_at),
                 [
                     (mid, tokens_local, 0, middle, first),
-                    (received, tokens_local, 0, count, 0),
+                    (received, tokens_local, 0, second_count, first - second_first),
                 ],
                 [
                     token_blocks(all_grads, (at, at + 1)),
                     token_blocks(shared, (at + 2, at + 3)),
                 ],
-                [(sign_bits, middle, first), (flips, middle - split, first - split)],
+                [(sign_bits, middle, first), (flips, count, 0)],
                 samples,
             )
 
-        second = after(second, near_sum)
-        end_one = send(middle_slice(mid, 1, groups, middle, 0, split), outward, near_sum)
-        end_two = send(second, outward)
-        far_sums = [own_far_piece(is_inner, mid, second)]
-        for index, cut in enumerate(far_cuts):
+        far_sums = []
+        done = near_sum
+        for index, flip in enumerate(flips):
+            received = seconds[index // 2]
+            far_sums.append(far_piece(index, after(received, done), after(flip, done)))
             done = far_sums[-1]
-            if index == len(far_cuts) - 1:
-                one, two = after(end_one, done), after(end_two, done)
-                far_sums.append(own_far_piece(1 - is_inner, one, two))
-                done = far_sums[-1]
-            far_sums.append(far_piece(*cut, after(seconds[index], done), after(flips, done)))
         far_sum = functools.reduce(jnp.add, far_sums)
         sums = jnp.where(
             near == 0, jnp.stack([near_sum, far_sum]), jnp.stack([far_sum, near_sum])

time: 279 us -> 262 us (0.939)
  starting transfers between devices: 34.4 us -> 68.8 us
  waiting for transfers between devices: 120 us -> 88.4 us
  Pallas kernels: 69.1 us -> 48.3 us
    ppermute x5, starting transfers between devices: 3.34 us -> 43.3 us  [sum_over(): value = value + lax.ppermute(value, axis, pairs)]
    ppermute x10 -> x8, waiting for transfers between devices: 97.3 us -> 75.2 us  [send(): return lax.ppermute(after(value, *earlier), 'narrow', pairs)]
    pallas_call x6 -> x4, Pallas kernels: 69.1 us -> 48.3 us  [piece(): pl.pallas_call(functools.partial(piece_kernel, len(acts), groups, [len(ea...]
    ppermute x10 -> x8, starting transfers between devices: 29.1 us -> 22.7 us  [send(): return lax.ppermute(after(value, *earlier), 'narrow', pairs)]
    ppermute x1, waiting for transfers between devices: 5.47 us -> 0.72 us  [shards(): first_part = lax.ppermute(out_grad[:depth], ('wide', 'narrow'), swaps[0])]
    ppermute x5, waiting for transfers between devices: 16.7 us -> 12.4 us  [sum_over(): value = value + lax.ppermute(value, axis, pairs)]
    slice x5 -> x4, local copies, waits for them, and re-layouts: 8.94 us -> 10.3 us  [middle_slice(): cuts.append(lax.slice_in_dim(array, start, start + count * BAND, axis=axis))]
  transfers between devices with their start and end apart: 19 -> 17, of which waited for: 9 -> 8; matrix products, arithmetic and copies ran while one was open for 12% -> 14% of each run, Pallas kernels for 23% -> 16%
where the time goes in v2:
time: 262 us; the launch traced here: 261 us
  waiting for transfers between devices  88.4 us (34%)
  starting transfers between devices  68.8 us (26%)
  Pallas kernels  48.3 us (18%)
  other arithmetic  24.9 us (10%)
  local copies, waits for them, and re-layouts  17.3 us (7%)
  between operations  13.6 us (5%)
    ppermute x8, waiting for transfers between devices, send(): return lax.ppermute(after(value, *earlier), 'narrow', pairs)  75.2 us
    pallas_call x4, Pallas kernels, piece(): pl.pallas_call(functools.partial(piece_kernel, len(acts), groups, [len(ea...  48.3 us
    ppermute x5, starting transfers between devices, sum_over(): value = value + lax.ppermute(value, axis, pairs)  43.3 us
    ppermute x8, starting transfers between devices, send(): return lax.ppermute(after(value, *earlier), 'narrow', pairs)  22.7 us
    ppermute x5, waiting for transfers between devices, sum_over(): value = value + lax.ppermute(value, axis, pairs)  12.4 us
    slice x4, local copies, waits for them, and re-layouts, middle_slice(): cuts.append(lax.slice_in_dim(array, start, start + count * BAND, axis=axis))  10.3 us
    sort x1, other arithmetic, ordered_samples(): lax.sort((pick_middle * picks + numbers, row_place * (2 * cols_local) + c...  6.88 us
  transfers between devices with their start and end apart: 17, of which 8 were waited for; matrix products, arithmetic and copies ran while one was open for 14% of the time, Pallas kernels for 16%

profile of v2, /device:TPU:0, one launch (start us, length us, event | category | flops | bytes accessed | tf_op | source)
XLA Modules:
  0.0 261.4 jit_solution(2306852017609168252)
XLA Ops:
  6.5 2.3 copy.10
  8.9 2.5 collective-permute-start.1
  11.4 4.1 %collective-permute-start = (bf16[1024,1792]{1,0:T(8,128)(2,1)}, bf16[1024,1792]{1,0:T(8,128)(2,1)}, u32[]{:S(2)}, u32[]{:S(2)}) collective-permute-start(bf16[1024,1792]{1,0:T(8,128)(2,1)} %refs_1_.1), channel_id=1, source_target_pairs={{0,1},{1,0},{2,3},{3,2},{4,5},{5,4},{6,7},{7,6},{8,9},{9,8},{10,11... | collective-permute-start | bytes 11010056 | tf_op jit(solution)/shard_map/ppermute | solution.py:308
  15.5 2.3 fusion.38
  20.7 6.9 %sort.23 = (s32[8192]{0:T(1024)S(1)}, s32[8192]{0:T(1024)S(1)}, s32[8192]{0:T(1024)}) sort(s32[8192]{0:T(1024)S(1)} %get-tuple-element.31, s32[8192]{0:T(1024)S(1)} %get-tuple-element.49, s32[8192]{0:T(1024)S(1)} %iota.23), dimensions={0}, to_apply=%region_1.2 | sort | flops 106496 | bytes 196608 | tf_op jit(solution)/shard_map/sort | solution.py:236
  27.8 4.0 %fusion.34 = (s32[384,1024]{1,0:T(8,128)}, s32[384,1024]{1,0:T(8,128)}) fusion(s32[1792,1024]{1,0:T(8,128)} %refs_17_.5), kind=kLoop, calls=%fused_computation.94 | loop fusion | bytes 6291456 | tf_op jit(solution)/shard_map/slice | solution.py:214
  32.0 3.7 %fusion.refs_12_.refs_22_ = bf16[8192,128]{1,0:T(8,128)(2,1)S(1)} fusion(s32[8192]{0:T(1024)S(1)} %get-tuple-element.46), kind=kLoop, calls=%fused_computation.2 | loop fusion | flops 2097152 | bytes 2129920 | tf_op jit(solution)/shard_map/convert_element_type | solution.py:254
  36.2 3.0 %fusion.35 = (s32[256,1024]{1,0:T(8,128)S(1)}, s32[256,1024]{1,0:T(8,128)S(1)}, s32[256,1024]{1,0:T(8,128)S(1)}, s32[256,1024]{1,0:T(8,128)S(1)}) fusion(s32[1792,1024]{1,0:T(8,128)} %refs_17_.5), kind=kLoop, calls=%fused_computation.95 | loop fusion | bytes 8388608 | tf_op jit(solution)/shard_map/slice | solution.py:214
  41.1 2.1 collective-permute-start.5
  43.2 1.6 fusion.2
  44.8 2.0 fusion.4
  46.9 58.4 %collective-permute-done.5 = bf16[1024,256]{1,0:T(8,128)(2,1)} collective-permute-done((bf16[1024,256]{1,0:T(8,128)(2,1)S(1)}, bf16[1024,256]{1,0:T(8,128)(2,1)}, u32[]{:S(2)}, u32[]{:S(2)}) %collective-permute-start.5) | collective-permute-done | bytes 524320 | tf_op jit(solution)/shard_map/ppermute | solution.py:308
  106.3 3.9 %subtract_convert_fusion.refs_10_.refs_20_ = bf16[256,8192]{1,0:T(8,128)(2,1)} fusion(s32[8192]{0:T(1024)S(1)} %get-tuple-element.52), kind=kLoop, calls=%fused_computation | loop fusion | flops 12582912 | bytes 4227072 | tf_op jit(solution)/shard_map/convert_element_type | solution.py:246
  110.1 5.5 %collective-permute-start.6 = (bf16[512,1024]{1,0:T(8,128)(2,1)}, bf16[512,1024]{1,0:T(8,128)(2,1)}, u32[]{:S(2)}, u32[]{:S(2)}) collective-permute-start(bf16[512,1024]{1,0:T(8,128)(2,1)} %get-tuple-element.23), channel_id=1, source_target_pairs={{0,1},{3,2},{4,5},{7,6},{8,9},{11,10},{12,13},{15,14},{16,17},{19,... | collective-permute-start | bytes 3145736 | tf_op jit(solution)/shard_map/ppermute | solution.py:308
  115.6 1.7 fusion.36
  117.3 1.7 pad_maximum_fusion
  119.0 2.0 collective-permute-start.2
  121.0 2.3 collective-permute-start.7
  123.3 2.5 collective-permute-start.9
  128.6 1.8 collective-permute-start.8
  131.4 32.8 %shard_map.64 = f32[64,128]{1,0:T(8,128)S(1)} custom-call(s32[11]{0:T(128)S(1)} %pad_add_fusion.scalars, bf16[1024,1792]{1,0:T(8,128)(2,1)} %refs_1_.1, bf16[1024,1792]{1,0:T(8,128)(2,1)} %refs_1_.1, bf16[1024,1792]{1,0:T(8,128)(2,1)} %collective-permute-done.refs_2_.refs_3_, bf16[1024,1792]{1,0:T(8,128)(2,1)} %collective-permute-done.refs_2_.refs_3_, ...), custom_call_target="tpu_custom_call" | custom-call | flops 30064771072 | bytes 262144 | tf_op jit(solution)/shard_map/pallas_call | solution.py:184
  165.3 5.1 %shard_map.65 = f32[64,128]{1,0:T(8,128)S(1)} custom-call(s32[8]{0:T(128)S(1)} %concatenate.30.scalars, bf16[1024,1792]{1,0:T(8,128)(2,1)} %collective-permute-done.1.refs_0_.refs_1_, bf16[1024,1792]{1,0:T(8,128)(2,1)} %collective-permute-done.1.refs_0_.refs_1_, bf16[1024,1024]{1,0:T(8,128)(2,1)} %collective-permute-done.2.refs_2_.refs_3_, ...), custom_call_target="tpu_custom_call" | custom-call | flops 17179869184 | bytes 524288 | tf_op jit(solution)/shard_map/pallas_call | solution.py:184
  170.4 5.1 %shard_map.66 = f32[64,128]{1,0:T(8,128)S(1)} custom-call(s32[8]{0:T(128)S(1)} %concatenate.33.scalars, bf16[1024,1792]{1,0:T(8,128)(2,1)} %collective-permute-done.1.refs_0_.refs_1_, bf16[1024,1792]{1,0:T(8,128)(2,1)} %collective-permute-done.1.refs_0_.refs_1_, bf16[1024,1024]{1,0:T(8,128)(2,1)} %collective-permute-done.2.refs_2_.refs_3_, ...), custom_call_target="tpu_custom_call" | custom-call | flops 17179869184 | bytes 524288 | tf_op jit(solution)/shard_map/pallas_call | solution.py:184
  175.5 16.8 %collective-permute-done.9.refs_18_.refs_19_ = bf16[768,1024]{1,0:T(8,128)(2,1)} collective-permute-done((bf16[768,1024]{1,0:T(8,128)(2,1)}, bf16[768,1024]{1,0:T(8,128)(2,1)}, u32[]{:S(2)}, u32[]{:S(2)}) %collective-permute-start.9) | collective-permute-done | bytes 1572896 | tf_op jit(solution)/shard_map/ppermute | solution.py:308
  192.3 5.4 %shard_map.67 = f32[64,128]{1,0:T(8,128)S(1)} custom-call(s32[9]{0:T(128)S(1)} %concatenate.35.scalars, bf16[1024,1792]{1,0:T(8,128)(2,1)} %collective-permute-done.1.refs_0_.refs_1_, bf16[1024,1792]{1,0:T(8,128)(2,1)} %collective-permute-done.1.refs_0_.refs_1_, bf16[1024,768]{1,0:T(8,128)(2,1)} %collective-permute-done.8.refs_2_.refs_3_, ...), custom_call_target="tpu_custom_call" | custom-call | flops 25769803776 | bytes 524288 | tf_op jit(solution)/shard_map/pallas_call | solution.py:184
  200.8 2.8 %collective-permute-done.11 = f32[2,8192]{1,0:T(2,128)S(1)} collective-permute-done((f32[2,8192]{1,0:T(2,128)S(1)}, f32[2,8192]{1,0:T(2,128)S(1)}, u32[]{:S(2)}, u32[]{:S(2)}) %collective-permute-start.11) | collective-permute-done | bytes 65568 | tf_op jit(solution)/shard_map/ppermute | solution.py:223
  203.7 1.6 collective-permute-start.12
  205.3 2.7 %collective-permute-done.12 = f32[2,8192]{1,0:T(2,128)S(1)} collective-permute-done((f32[2,8192]{1,0:T(2,128)S(1)}, f32[2,8192]{1,0:T(2,128)S(1)}, u32[]{:S(2)}, u32[]{:S(2)}) %collective-permute-start.12) | collective-permute-done | bytes 65568 | tf_op jit(solution)/shard_map/ppermute | solution.py:223
  208.1 38.1 %collective-permute-start.13 = (f32[2,8192]{1,0:T(2,128)S(1)}, f32[2,8192]{1,0:T(2,128)S(1)}, u32[]{:S(2)}, u32[]{:S(2)}) collective-permute-start(f32[2,8192]{1,0:T(2,128)S(1)} %add.132), channel_id=1, source_target_pairs={{0,1},{1,0},{2,3},{3,2},{4,5},{5,4},{6,7},{7,6},{8,9},{9,8},{10,11... | collective-permute-start | bytes 196616 | tf_op jit(solution)/shard_map/ppermute | solution.py:223
  246.2 2.4 collective-permute-done.13
  248.7 2.0 collective-permute-start.14
  250.6 3.3 %collective-permute-done.14 = f32[2,8192]{1,0:T(2,128)S(1)} collective-permute-done((f32[2,8192]{1,0:T(2,128)S(1)}, f32[2,8192]{1,0:T(2,128)S(1)}, u32[]{:S(2)}, u32[]{:S(2)}) %collective-permute-start.14) | collective-permute-done | bytes 65568 | tf_op jit(solution)/shard_map/ppermute | solution.py:223
  (60 shorter events, 15.7 us)
Async XLA Ops:
  6.5 14.0 %copy-start.7 = (s32[8192]{0:T(1024)S(1)}, s32[8192]{0:T(1024)}, u32[]{:S(2)}) copy-start(s32[8192]{0:T(1024)} %param.10) | copy-start | bytes 98308
  6.5 14.0 %copy-start.6 = (s32[8192]{0:T(1024)S(1)}, s32[8192]{0:T(1024)}, u32[]{:S(2)}) copy-start(s32[8192]{0:T(1024)} %param.9) | copy-start | bytes 98308
  6.5 123.8 %all-gather.3.cloned.1.call-start = ((), (), s32[]{:S(2)}) async-start(), calls=%async_computation | async-start | bytes 9437184 | tf_op jit(solution)/shard_map/all_gather | solution.py:290
  8.9 155.4 %all-gather.5.cloned.1.call-start = ((), (), s32[]{:S(2)}) async-start(), calls=%async_computation.1 | async-start | bytes 4718592 | tf_op jit(solution)/shard_map/all_gather | solution.py:313
  8.9 101.2 %collective-permute-start.1 = (bf16[1024,1792]{1,0:T(8,128)(2,1)}, bf16[1024,1792]{1,0:T(8,128)(2,1)}, u32[]{:S(2)}, u32[]{:S(2)}) collective-permute-start(bf16[1024,1792]{1,0:T(8,128)(2,1)} %refs_1_.1), channel_id=1, source_target_pairs={{1,2},{2,1},{5,6},{6,5},{9,10},{10,9},{13,14},{14,13},{17,18},{18,... | collective-permute-start | bytes 11010056 | tf_op jit(solution)/shard_map/ppermute | solution.py:308
  11.4 98.8 %collective-permute-start = (bf16[1024,1792]{1,0:T(8,128)(2,1)}, bf16[1024,1792]{1,0:T(8,128)(2,1)}, u32[]{:S(2)}, u32[]{:S(2)}) collective-permute-start(bf16[1024,1792]{1,0:T(8,128)(2,1)} %refs_1_.1), channel_id=1, source_target_pairs={{0,1},{1,0},{2,3},{3,2},{4,5},{5,4},{6,7},{7,6},{8,9},{9,8},{10,11... | collective-permute-start | bytes 11010056 | tf_op jit(solution)/shard_map/ppermute | solution.py:308
  17.8 22.2 %collective-permute-start.3 = (bf16[256,1024]{0,1:T(8,128)(2,1)}, bf16[256,1024]{0,1:T(8,128)(2,1)}, u32[]{:S(2)}, u32[]{:S(2)}) collective-permute-start(bf16[256,1024]{0,1:T(8,128)(2,1)} %get-tuple-element.44), channel_id=1, source_target_pairs={{16,0},{20,8},{24,16},{28,24},{17,1},{21,9},{25,17},{29,25},{2,2},... | collective-permute-start | bytes 1572872 | tf_op jit(solution)/shard_map/ppermute | solution.py:299
  19.1 20.9 %collective-permute-start.4 = (bf16[256,1024]{0,1:T(8,128)(2,1)}, bf16[256,1024]{0,1:T(8,128)(2,1)}, u32[]{:S(2)}, u32[]{:S(2)}) collective-permute-start(bf16[256,1024]{0,1:T(8,128)(2,1)} %get-tuple-element.43), channel_id=1, source_target_pairs={{16,4},{20,12},{24,20},{28,28},{17,5},{21,13},{25,21},{29,29},{2,6... | collective-permute-start | bytes 1572872 | tf_op jit(solution)/shard_map/ppermute | solution.py:300
  35.7 94.7 %copy-start = (bf16[8192,128]{1,0:T(8,128)(2,1)}, bf16[8192,128]{1,0:T(8,128)(2,1)S(1)}, u32[]{:S(2)}) copy-start(bf16[8192,128]{1,0:T(8,128)(2,1)S(1)} %fusion.refs_12_.refs_22_) | copy-start | bytes 6291460
  36.2 7.0 %copy-start.4 = (s32[384,1024]{1,0:T(8,128)S(1)}, s32[384,1024]{1,0:T(8,128)}, u32[]{:S(2)}) copy-start(s32[384,1024]{1,0:T(8,128)} %get-tuple-element.33) | copy-start | bytes 4718596
  36.2 7.0 %copy-start.5 = (s32[384,1024]{1,0:T(8,128)S(1)}, s32[384,1024]{1,0:T(8,128)}, u32[]{:S(2)}) copy-start(s32[384,1024]{1,0:T(8,128)} %get-tuple-element.34) | copy-start | bytes 4718596
  41.1 64.2 %collective-permute-start.5 = (bf16[1024,256]{1,0:T(8,128)(2,1)S(1)}, bf16[1024,256]{1,0:T(8,128)(2,1)}, u32[]{:S(2)}, u32[]{:S(2)}) collective-permute-start(bf16[1024,256]{1,0:T(8,128)(2,1)S(1)} %select_bitcast_fusion), channel_id=1, source_target_pairs={{0,1},{3,2},{4,5},{7,6},{8,9},{11,10},{12,13},{15,14},{16,17},{19,... | collective-permute-start | bytes 1572872 | tf_op jit(solution)/shard_map/ppermute | solution.py:308
  44.8 60.5 %copy-start.8 = (s32[16]{0:T(128)S(1)}, s32[16]{0:T(128)}, u32[]{:S(2)}) copy-start(s32[16]{0:T(128)} %constant.197.clone) | copy-start | bytes 196
  110.1 54.1 %collective-permute-start.6 = (bf16[512,1024]{1,0:T(8,128)(2,1)}, bf16[512,1024]{1,0:T(8,128)(2,1)}, u32[]{:S(2)}, u32[]{:S(2)}) collective-permute-start(bf16[512,1024]{1,0:T(8,128)(2,1)} %get-tuple-element.23), channel_id=1, source_target_pairs={{0,1},{3,2},{4,5},{7,6},{8,9},{11,10},{12,13},{15,14},{16,17},{19,... | collective-permute-start | bytes 3145736 | tf_op jit(solution)/shard_map/ppermute | solution.py:308
  119.0 45.3 %collective-permute-start.2 = (bf16[1024,1024]{1,0:T(8,128)(2,1)}, bf16[1024,1024]{1,0:T(8,128)(2,1)}, u32[]{:S(2)}, u32[]{:S(2)}) collective-permute-start(bf16[1024,1024]{1,0:T(8,128)(2,1)} %pad_maximum_fusion), channel_id=1, source_target_pairs={{1,2},{2,1},{5,6},{6,5},{9,10},{10,9},{13,14},{14,13},{17,18},{18,... | collective-permute-start | bytes 6291464 | tf_op jit(solution)/shard_map/ppermute | solution.py:308
  121.0 49.5 %collective-permute-start.7 = (bf16[512,1024]{1,0:T(8,128)(2,1)}, bf16[512,1024]{1,0:T(8,128)(2,1)}, u32[]{:S(2)}, u32[]{:S(2)}) collective-permute-start(bf16[512,1024]{1,0:T(8,128)(2,1)} %get-tuple-element.26), channel_id=1, source_target_pairs={{0,1},{3,2},{4,5},{7,6},{8,9},{11,10},{12,13},{15,14},{16,17},{19,... | collective-permute-start | bytes 3145736 | tf_op jit(solution)/shard_map/ppermute | solution.py:308
  123.3 69.0 %collective-permute-start.9 = (bf16[768,1024]{1,0:T(8,128)(2,1)}, bf16[768,1024]{1,0:T(8,128)(2,1)}, u32[]{:S(2)}, u32[]{:S(2)}) collective-permute-start(bf16[768,1024]{1,0:T(8,128)(2,1)} %fusion.2), channel_id=1, source_target_pairs={{0,1},{3,2},{4,5},{7,6},{8,9},{11,10},{12,13},{15,14},{16,17},{19,... | collective-permute-start | bytes 4718600 | tf_op jit(solution)/shard_map/ppermute | solution.py:308
  128.6 63.8 %collective-permute-start.8 = (bf16[1024,768]{1,0:T(8,128)(2,1)}, bf16[1024,768]{1,0:T(8,128)(2,1)}, u32[]{:S(2)}, u32[]{:S(2)}) collective-permute-start(bf16[1024,768]{1,0:T(8,128)(2,1)} %pad_maximum_fusion.1), channel_id=1, source_target_pairs={{1,2},{2,1},{5,6},{6,5},{9,10},{10,9},{13,14},{14,13},{17,18},{18,... | collective-permute-start | bytes 4718600 | tf_op jit(solution)/shard_map/ppermute | solution.py:308
  130.4 1.0 copy-start.1
  164.3 1.0 copy-start.2
  170.4 21.9 %copy-start.3 = (f32[16,8192]{1,0:T(8,128)S(1)}, f32[16,8192]{1,0:T(8,128)}, u32[]{:S(2)}) copy-start(f32[16,8192]{1,0:T(8,128)} %subtract_convert_fusion.1.refs_11_.refs_21_) | copy-start | bytes 1572868
  197.8 1.3 collective-permute-start.10
  199.3 4.3 %collective-permute-start.11 = (f32[2,8192]{1,0:T(2,128)S(1)}, f32[2,8192]{1,0:T(2,128)S(1)}, u32[]{:S(2)}, u32[]{:S(2)}) collective-permute-start(f32[2,8192]{1,0:T(2,128)S(1)} %fusion.40), channel_id=1, source_target_pairs={{0,8},{4,12},{8,0},{12,4},{16,24},{20,28},{24,16},{28,20},{1,9},{5... | collective-permute-start | bytes 196616 | tf_op jit(solution)/shard_map/ppermute | solution.py:223
  203.7 4.3 %collective-permute-start.12 = (f32[2,8192]{1,0:T(2,128)S(1)}, f32[2,8192]{1,0:T(2,128)S(1)}, u32[]{:S(2)}, u32[]{:S(2)}) collective-permute-start(f32[2,8192]{1,0:T(2,128)S(1)} %fusion.41), channel_id=1, source_target_pairs={{0,16},{4,20},{8,24},{12,28},{16,0},{20,4},{24,8},{28,12},{1,17},{... | collective-permute-start | bytes 196616 | tf_op jit(solution)/shard_map/ppermute | solution.py:223
  208.1 40.5 %collective-permute-start.13 = (f32[2,8192]{1,0:T(2,128)S(1)}, f32[2,8192]{1,0:T(2,128)S(1)}, u32[]{:S(2)}, u32[]{:S(2)}) collective-permute-start(f32[2,8192]{1,0:T(2,128)S(1)} %add.132), channel_id=1, source_target_pairs={{0,1},{1,0},{2,3},{3,2},{4,5},{5,4},{6,7},{7,6},{8,9},{9,8},{10,11... | collective-permute-start | bytes 196616 | tf_op jit(solution)/shard_map/ppermute | solution.py:223
  248.7 5.2 %collective-permute-start.14 = (f32[2,8192]{1,0:T(2,128)S(1)}, f32[2,8192]{1,0:T(2,128)S(1)}, u32[]{:S(2)}, u32[]{:S(2)}) collective-permute-start(f32[2,8192]{1,0:T(2,128)S(1)} %add.133), channel_id=1, source_target_pairs={{0,2},{1,3},{2,0},{3,1},{4,6},{5,7},{6,4},{7,5},{8,10},{9,11},{10,... | collective-permute-start | bytes 196616 | tf_op jit(solution)/shard_map/ppermute | solution.py:223
Sparse Core Ops, SparseCore 0:
  9.2 66.1 all-gather.2
  105.4 36.9 all-gather.4

commit v3 on v2

--- a/solution.py
+++ b/solution.py
@@ -315,10 +315,25 @@
         def paired_part(first, count):
             return middle_slice(paired, 1, groups, middle, first, count)
 
-        far_cuts = [(0, 2), (2, 2), (4, middle - 4)]
-        second_cuts = [(0, 4), far_cuts[2]]
-        seconds = [send(paired_part(*cut), inner) for cut in second_cuts]
-        flips = [send(far_signs(*cut), inward, paired) for cut in far_cuts]
+        far_cuts = [(0, 2), (2, middle - 4), (middle - 2, 2)]
+        near_cuts = [(0, middle - 2), (middle - 2, 2)]
+        ends = [middle_slice(hidden, 1, groups, middle, *cut) for cut in near_cuts]
+        mids = [send(end, inner) for end in ends]
+        paired = [after(send(ends[0], partner), mids[0])]
+        paired.append(send(ends[1], partner, paired[0]))
+
+        def cut_of(index):
+            first, _ = far_cuts[index]
+            which = 0 if first < near_cuts[1][0] else 1
+            offset, size = near_cuts[which]
+            return which, size, first - offset
+
+        def second_part(index):
+            which, size, place = cut_of(index)
+            return middle_slice(paired[which], 1, groups, size, place, far_cuts[index][1])
+
+        seconds = [send(second_part(index), inner) for index in (0, 1)]
+        flips = [send(far_signs(*cut), inward, paired[0]) for cut in far_cuts[:2]]
 
         shared_tokens = share.shape[1]
 
@@ -333,21 +348,33 @@
         def first_of(tokens, block):
             return block * (tokens_local // tokens)
 
-        near_sum = piece(
-            middle,
-            groups,
-            scalars(
-                1,
-                0,
-                middle,
-                first_of(tokens, narrow_index),
-                first_of(tokens, narrow_index ^ 1),
-            ),
-            [(hidden, tokens_local, 0, middle, 0), (paired, tokens_local, 0, middle, 0)],
-            [token_blocks(all_grads, (middle + 2, middle + 3))],
-            [(sign_bits, middle, 0)],
-            samples,
-        )
+        def near_piece(index, received):
+            first, count = near_cuts[index]
+            return piece(
+                count,
+                groups,
+                scalars(
+                    1,
+                    first,
+                    count,
+                    first_of(tokens, narrow_index),
+                    first_of(tokens, narrow_index ^ 1),
+                ),
+                [
+                    (hidden, tokens_local, 0, middle, first),
+                    (received, tokens_local, 0, count, 0),
+                ],
+                [token_blocks(all_grads, (count + 2, count + 3))],
+                [(sign_bits, middle, first)],
+                samples,
+            )
+
+        near_first = near_piece(0, after(paired[0], mids[1]))
+        paired[1] = after(paired[1], near_first)
+        seconds.append(send(second_part(2), inner))
+        flips.append(send(far_signs(*far_cuts[2]), inward, paired[1]))
+        near_second = near_piece(1, paired[1])
+        near_sum = near_first + near_second
 
         far_one = 2 - near
         far_two = far_one ^ 1
@@ -361,15 +388,15 @@
 
         def far_piece(index, received, flips):
             first, count = far_cuts[index]
-            second_first, second_count = second_cuts[index // 2]
+            which, size, place = cut_of(index)
             at = count + 2
             return piece(
                 count,
                 groups,
                 scalars(is_inner, first, count, *far_at),
                 [
-                    (mid, tokens_local, 0, middle, first),
-                    (received, tokens_local, 0, second_count, first - second_first),
+                    (mids[which], tokens_local, 0, size, place),
+                    (received, tokens_local, 0, count, 0),
                 ],
                 [
                     token_blocks(all_grads, (at, at + 1)),
@@ -380,10 +407,10 @@
             )
 
         far_sums = []
-        done = near_sum
+        done = near_second
         for index, flip in enumerate(flips):
-            received = seconds[index // 2]
-            far_sums.append(far_piece(index, after(received, done), after(flip, done)))
+            received = after(seconds[index], done)
+            far_sums.append(far_piece(index, received, after(flip, done)))
             done = far_sums[-1]
         far_sum = functools.reduce(jnp.add, far_sums)
         sums = jnp.where(

time: 262 us -> 257 us (0.981)
  waiting for transfers between devices: 88.4 us -> 81.3 us
  Pallas kernels: 48.3 us -> 52.7 us
  starting transfers between devices: 68.8 us -> 65.1 us
    ppermute x5, starting transfers between devices: 43.3 us -> 29.2 us  [sum_over(): value = value + lax.ppermute(value, axis, pairs)]
    ppermute x8 -> x11, starting transfers between devices: 22.7 us -> 33.1 us  [send(): return lax.ppermute(after(value, *earlier), 'narrow', pairs)]
    ppermute x8 -> x11, waiting for transfers between devices: 75.2 us -> 68.5 us  [send(): return lax.ppermute(after(value, *earlier), 'narrow', pairs)]
    pallas_call x4 -> x5, Pallas kernels: 48.3 us -> 52.7 us  [piece(): pl.pallas_call(functools.partial(piece_kernel, len(acts), groups, [len(ea...]
    slice x4 -> x6, local copies, waits for them, and re-layouts: 10.3 us -> 11.2 us  [middle_slice(): cuts.append(lax.slice_in_dim(array, start, start + count * BAND, axis=axis))]
  transfers between devices with their start and end apart: 17 -> 20, of which waited for: 8 -> 8; matrix products, arithmetic and copies ran while one was open for 14% -> 15% of each run, Pallas kernels for 16% -> 19%
where the time goes in v3:
time: 257 us
  waiting for transfers between devices  81.3 us (32%)
  starting transfers between devices  65.1 us (25%)
  Pallas kernels  52.7 us (21%)
  other arithmetic  26.1 us (10%)
  local copies, waits for them, and re-layouts  17.7 us (7%)
  between operations  13.7 us (5%)
    ppermute x11, waiting for transfers between devices, send(): return lax.ppermute(after(value, *earlier), 'narrow', pairs)  68.5 us
    pallas_call x5, Pallas kernels, piece(): pl.pallas_call(functools.partial(piece_kernel, len(acts), groups, [len(ea...  52.7 us
    ppermute x11, starting transfers between devices, send(): return lax.ppermute(after(value, *earlier), 'narrow', pairs)  33.1 us
    ppermute x5, starting transfers between devices, sum_over(): value = value + lax.ppermute(value, axis, pairs)  29.2 us
    ppermute x5, waiting for transfers between devices, sum_over(): value = value + lax.ppermute(value, axis, pairs)  12.7 us
    slice x6, local copies, waits for them, and re-layouts, middle_slice(): cuts.append(lax.slice_in_dim(array, start, start + count * BAND, axis=axis))  11.2 us
    sort x1, other arithmetic, ordered_samples(): lax.sort((pick_middle * picks + numbers, row_place * (2 * cols_local) + c...  6.88 us
    unnamed x21, local copies, waits for them, and re-layouts  5.18 us
  transfers between devices with their start and end apart: 20, of which 8 were waited for; matrix products, arithmetic and copies ran while one was open for 15% of the time, Pallas kernels for 19%

profile of v3, /device:TPU:0, one launch (start us, length us, event | category | flops | bytes accessed | tf_op | source)
XLA Modules:
  0.0 256.7 jit_solution(18296876961334827241)
XLA Ops:
  6.5 2.3 copy.10
  8.9 1.9 fusion.36
  10.8 1.7 pad_maximum_fusion
  12.5 2.3 collective-permute-start.1
  14.8 4.4 %collective-permute-start = (bf16[1024,1280]{1,0:T(8,128)(2,1)}, bf16[1024,1280]{1,0:T(8,128)(2,1)}, u32[]{:S(2)}, u32[]{:S(2)}) collective-permute-start(bf16[1024,1280]{1,0:T(8,128)(2,1)} %pad_maximum_fusion), channel_id=1, source_target_pairs={{0,1},{1,0},{2,3},{3,2},{4,5},{5,4},{6,7},{7,6},{8,9},{9,8},{10,11... | collective-permute-start | bytes 7864328 | tf_op jit(solution)/shard_map/ppermute | solution.py:308
  21.7 1.7 collective-permute-start.2
  27.2 6.9 %sort.23 = (s32[8192]{0:T(1024)S(1)}, s32[8192]{0:T(1024)S(1)}, s32[8192]{0:T(1024)}) sort(s32[8192]{0:T(1024)S(1)} %get-tuple-element.37, s32[8192]{0:T(1024)S(1)} %get-tuple-element.59, s32[8192]{0:T(1024)S(1)} %iota.23), dimensions={0}, to_apply=%region_1.2 | sort | flops 106496 | bytes 196608 | tf_op jit(solution)/shard_map/sort | solution.py:236
  34.1 3.9 %subtract_convert_fusion.refs_10_.refs_20_ = bf16[256,8192]{1,0:T(8,128)(2,1)} fusion(s32[8192]{0:T(1024)S(1)} %get-tuple-element.62), kind=kLoop, calls=%fused_computation | loop fusion | flops 12582912 | bytes 4227072 | tf_op jit(solution)/shard_map/convert_element_type | solution.py:246
  38.1 3.7 %fusion.refs_12_.refs_22_ = bf16[8192,128]{1,0:T(8,128)(2,1)S(1)} fusion(s32[8192]{0:T(1024)S(1)} %get-tuple-element.56), kind=kLoop, calls=%fused_computation.2 | loop fusion | flops 2097152 | bytes 2129920 | tf_op jit(solution)/shard_map/convert_element_type | solution.py:254
  42.1 4.0 %collective-permute-start.7 = (bf16[1024,256]{1,0:T(8,128)(2,1)S(1)}, bf16[1024,256]{1,0:T(8,128)(2,1)S(1)}, u32[]{:S(2)}, u32[]{:S(2)}) collective-permute-start(bf16[1024,256]{1,0:T(8,128)(2,1)S(1)} %select_bitcast_fusion), channel_id=1, source_target_pairs={{0,1},{3,2},{4,5},{7,6},{8,9},{11,10},{12,13},{15,14},{16,17},{19,... | collective-permute-start | bytes 1572872 | tf_op jit(solution)/shard_map/ppermute | solution.py:308
  46.5 2.3 fusion.35
  50.4 36.2 %collective-permute-done.7 = bf16[1024,256]{1,0:T(8,128)(2,1)S(1)} collective-permute-done((bf16[1024,256]{1,0:T(8,128)(2,1)S(1)}, bf16[1024,256]{1,0:T(8,128)(2,1)S(1)}, u32[]{:S(2)}, u32[]{:S(2)}) %collective-permute-start.7) | collective-permute-done | bytes 524320 | tf_op jit(solution)/shard_map/ppermute | solution.py:308
  87.6 2.7 %fusion.34 = (s32[256,1024]{1,0:T(8,128)S(1)}, s32[256,1024]{1,0:T(8,128)S(1)}, s32[256,1024]{1,0:T(8,128)S(1)}, s32[256,1024]{1,0:T(8,128)S(1)}) fusion(s32[1792,1024]{1,0:T(8,128)} %refs_17_.5), kind=kLoop, calls=%fused_computation.97 | loop fusion | bytes 8388608 | tf_op jit(solution)/shard_map/slice | solution.py:214
  90.4 1.9 fusion.4
  93.4 5.5 %collective-permute-start.3 = (bf16[1024,512]{1,0:T(8,128)(2,1)}, bf16[1024,512]{1,0:T(8,128)(2,1)}, u32[]{:S(2)}, u32[]{:S(2)}) collective-permute-start(bf16[1024,512]{1,0:T(8,128)(2,1)} %pad_maximum_fusion.2), channel_id=1, source_target_pairs={{0,1},{1,0},{2,3},{3,2},{4,5},{5,4},{6,7},{7,6},{8,9},{9,8},{10,11... | collective-permute-start | bytes 3145736 | tf_op jit(solution)/shard_map/ppermute | solution.py:308
  99.0 2.9 %collective-permute-start.8 = (bf16[512,1024]{1,0:T(8,128)(2,1)}, bf16[512,1024]{1,0:T(8,128)(2,1)}, u32[]{:S(2)}, u32[]{:S(2)}) collective-permute-start(bf16[512,1024]{1,0:T(8,128)(2,1)} %get-tuple-element.29), channel_id=1, source_target_pairs={{0,1},{3,2},{4,5},{7,6},{8,9},{11,10},{12,13},{15,14},{16,17},{19,... | collective-permute-start | bytes 3145736 | tf_op jit(solution)/shard_map/ppermute | solution.py:308
  105.8 3.3 %collective-permute-start.10 = (bf16[768,1024]{1,0:T(8,128)(2,1)}, bf16[768,1024]{1,0:T(8,128)(2,1)}, u32[]{:S(2)}, u32[]{:S(2)}) collective-permute-start(bf16[768,1024]{1,0:T(8,128)(2,1)} %fusion.2), channel_id=1, source_target_pairs={{0,1},{3,2},{4,5},{7,6},{8,9},{11,10},{12,13},{15,14},{16,17},{19,... | collective-permute-start | bytes 4718600 | tf_op jit(solution)/shard_map/ppermute | solution.py:308
  112.0 1.9 collective-permute-start.9
  115.0 25.0 %shard_map.64 = f32[64,128]{1,0:T(8,128)S(1)} custom-call(s32[9]{0:T(128)S(1)} %pad_add_fusion.scalars, bf16[1024,1792]{1,0:T(8,128)(2,1)} %refs_1_.3, bf16[1024,1792]{1,0:T(8,128)(2,1)} %refs_1_.3, bf16[1024,1280]{1,0:T(8,128)(2,1)} %collective-permute-done.refs_2_.refs_3_, bf16[1024,1280]{1,0:T(8,128)(2,1)} %collective-permute-done.refs_2_.refs_3_, ...), custom_call_target="tpu_custom_call" | custom-call | flops 21474836480 | bytes 262144 | tf_op jit(solution)/shard_map/pallas_call | solution.py:184
  140.0 12.6 %shard_map.65 = f32[64,128]{1,0:T(8,128)S(1)} custom-call(s32[6]{0:T(128)S(1)} %pad_add_fusion.1.scalars, bf16[1024,1792]{1,0:T(8,128)(2,1)} %refs_1_.3, bf16[1024,1792]{1,0:T(8,128)(2,1)} %refs_1_.3, bf16[1024,512]{1,0:T(8,128)(2,1)} %collective-permute-done.3.refs_2_.refs_3_, bf16[1024,512]{1,0:T(8,128)(2,1)} %collective-permute-done.3.refs_2_.refs_3_, ...), custom_call_target="tpu_custom_call" | custom-call | flops 8589934592 | bytes 262144 | tf_op jit(solution)/shard_map/pallas_call | solution.py:184
  153.7 5.1 %shard_map.66 = f32[64,128]{1,0:T(8,128)S(1)} custom-call(s32[8]{0:T(128)S(1)} %concatenate.43.scalars, bf16[1024,1280]{1,0:T(8,128)(2,1)} %collective-permute-done.1.refs_0_.refs_1_, bf16[1024,1280]{1,0:T(8,128)(2,1)} %collective-permute-done.1.refs_0_.refs_1_, bf16[1024,512]{1,0:T(8,128)(2,1)} %collective-permute-done.4.refs_2_.refs_3_, ...), custom_call_target="tpu_custom_call" | custom-call | flops 17179869184 | bytes 524288 | tf_op jit(solution)/shard_map/pallas_call | solution.py:184
  158.8 18.2 %collective-permute-done.10.refs_18_.refs_19_ = bf16[768,1024]{1,0:T(8,128)(2,1)} collective-permute-done((bf16[768,1024]{1,0:T(8,128)(2,1)}, bf16[768,1024]{1,0:T(8,128)(2,1)}, u32[]{:S(2)}, u32[]{:S(2)}) %collective-permute-start.10) | collective-permute-done | bytes 1572896 | tf_op jit(solution)/shard_map/ppermute | solution.py:308
  177.0 4.6 %collective-permute-start.12 = (bf16[512,1024]{1,0:T(8,128)(2,1)S(1)}, bf16[512,1024]{1,0:T(8,128)(2,1)S(1)}, u32[]{:S(2)}, u32[]{:S(2)}) collective-permute-start(bf16[512,1024]{1,0:T(8,128)(2,1)S(1)} %copy-done.5), channel_id=1, source_target_pairs={{0,1},{3,2},{4,5},{7,6},{8,9},{11,10},{12,13},{15,14},{16,17},{19,... | collective-permute-start | bytes 3145736 | tf_op jit(solution)/shard_map/ppermute | solution.py:308
  182.6 5.4 %shard_map.67 = f32[64,128]{1,0:T(8,128)S(1)} custom-call(s32[9]{0:T(128)S(1)} %concatenate.46.scalars, bf16[1024,1280]{1,0:T(8,128)(2,1)} %collective-permute-done.1.refs_0_.refs_1_, bf16[1024,1280]{1,0:T(8,128)(2,1)} %collective-permute-done.1.refs_0_.refs_1_, bf16[1024,768]{1,0:T(8,128)(2,1)} %collective-permute-done.9.refs_2_.refs_3_, ...), custom_call_target="tpu_custom_call" | custom-call | flops 25769803776 | bytes 524288 | tf_op jit(solution)/shard_map/pallas_call | solution.py:184
  188.0 14.2 %collective-permute-done.12.refs_18_.refs_19_ = bf16[512,1024]{1,0:T(8,128)(2,1)S(1)} collective-permute-done((bf16[512,1024]{1,0:T(8,128)(2,1)S(1)}, bf16[512,1024]{1,0:T(8,128)(2,1)S(1)}, u32[]{:S(2)}, u32[]{:S(2)}) %collective-permute-start.12) | collective-permute-done | bytes 1048608 | tf_op jit(solution)/shard_map/ppermute | solution.py:308
  202.1 4.6 %shard_map.68 = f32[64,128]{1,0:T(8,128)S(1)} custom-call(s32[8]{0:T(128)S(1)} %concatenate.49.scalars, bf16[1024,512]{1,0:T(8,128)(2,1)} %collective-permute-done.2.refs_0_.refs_1_, bf16[1024,512]{1,0:T(8,128)(2,1)} %collective-permute-done.2.refs_0_.refs_1_, bf16[1024,512]{1,0:T(8,128)(2,1)S(1)} %collective-permute-done.11.refs_2_.refs_3_, ...), custom_call_target="tpu_custom_call" | custom-call | flops 17179869184 | bytes 524288 | tf_op jit(solution)/shard_map/pallas_call | solution.py:184
  209.9 2.8 %collective-permute-done.14 = f32[2,8192]{1,0:T(2,128)S(1)} collective-permute-done((f32[2,8192]{1,0:T(2,128)S(1)}, f32[2,8192]{1,0:T(2,128)S(1)}, u32[]{:S(2)}, u32[]{:S(2)}) %collective-permute-start.14) | collective-permute-done | bytes 65568 | tf_op jit(solution)/shard_map/ppermute | solution.py:223
  214.4 2.7 %collective-permute-done.15 = f32[2,8192]{1,0:T(2,128)S(1)} collective-permute-done((f32[2,8192]{1,0:T(2,128)S(1)}, f32[2,8192]{1,0:T(2,128)S(1)}, u32[]{:S(2)}, u32[]{:S(2)}) %collective-permute-start.15) | collective-permute-done | bytes 65568 | tf_op jit(solution)/shard_map/ppermute | solution.py:223
  217.1 24.3 %collective-permute-start.16 = (f32[2,8192]{1,0:T(2,128)S(1)}, f32[2,8192]{1,0:T(2,128)S(1)}, u32[]{:S(2)}, u32[]{:S(2)}) collective-permute-start(f32[2,8192]{1,0:T(2,128)S(1)} %add.136), channel_id=1, source_target_pairs={{0,1},{1,0},{2,3},{3,2},{4,5},{5,4},{6,7},{7,6},{8,9},{9,8},{10,11... | collective-permute-start | bytes 196616 | tf_op jit(solution)/shard_map/ppermute | solution.py:223
  241.4 2.5 collective-permute-done.16
  243.9 1.7 collective-permute-start.17
  245.7 3.5 %collective-permute-done.17 = f32[2,8192]{1,0:T(2,128)S(1)} collective-permute-done((f32[2,8192]{1,0:T(2,128)S(1)}, f32[2,8192]{1,0:T(2,128)S(1)}, u32[]{:S(2)}, u32[]{:S(2)}) %collective-permute-start.17) | collective-permute-done | bytes 65568 | tf_op jit(solution)/shard_map/ppermute | solution.py:223
  (75 shorter events, 26.4 us)
Async XLA Ops:
  6.5 107.4 %all-gather.3.cloned.1.call-start = ((), (), s32[]{:S(2)}) async-start(), calls=%async_computation | async-start | bytes 9437184 | tf_op jit(solution)/shard_map/all_gather | solution.py:290
  8.8 143.8 %all-gather.5.cloned.1.call-start = ((), (), s32[]{:S(2)}) async-start(), calls=%async_computation.1 | async-start | bytes 4718592 | tf_op jit(solution)/shard_map/all_gather | solution.py:313
  12.5 10.9 %copy-start.4 = (bf16[512,1024]{0,1:T(8,128)(2,1)S(1)}, bf16[512,1024]{0,1:T(8,128)(2,1)}, u32[]{:S(2)}) copy-start(bf16[512,1024]{0,1:T(8,128)(2,1)} %copy.10) | copy-start | bytes 3145732
  12.5 80.9 %collective-permute-start.1 = (bf16[1024,1280]{1,0:T(8,128)(2,1)}, bf16[1024,1280]{1,0:T(8,128)(2,1)}, u32[]{:S(2)}, u32[]{:S(2)}) collective-permute-start(bf16[1024,1280]{1,0:T(8,128)(2,1)} %pad_maximum_fusion), channel_id=1, source_target_pairs={{1,2},{2,1},{5,6},{6,5},{9,10},{10,9},{13,14},{14,13},{17,18},{18,... | collective-permute-start | bytes 7864328 | tf_op jit(solution)/shard_map/ppermute | solution.py:308
  14.8 78.6 %collective-permute-start = (bf16[1024,1280]{1,0:T(8,128)(2,1)}, bf16[1024,1280]{1,0:T(8,128)(2,1)}, u32[]{:S(2)}, u32[]{:S(2)}) collective-permute-start(bf16[1024,1280]{1,0:T(8,128)(2,1)} %pad_maximum_fusion), channel_id=1, source_target_pairs={{0,1},{1,0},{2,3},{3,2},{4,5},{5,4},{6,7},{7,6},{8,9},{9,8},{10,11... | collective-permute-start | bytes 7864328 | tf_op jit(solution)/shard_map/ppermute | solution.py:308
  20.6 6.4 %copy-start.7 = (s32[8192]{0:T(1024)S(1)}, s32[8192]{0:T(1024)}, u32[]{:S(2)}) copy-start(s32[8192]{0:T(1024)} %param.9) | copy-start | bytes 98308
  20.6 6.4 %copy-start.8 = (s32[8192]{0:T(1024)S(1)}, s32[8192]{0:T(1024)}, u32[]{:S(2)}) copy-start(s32[8192]{0:T(1024)} %param.10) | copy-start | bytes 98308
  21.7 71.7 %collective-permute-start.2 = (bf16[1024,512]{1,0:T(8,128)(2,1)}, bf16[1024,512]{1,0:T(8,128)(2,1)}, u32[]{:S(2)}, u32[]{:S(2)}) collective-permute-start(bf16[1024,512]{1,0:T(8,128)(2,1)} %pad_maximum_fusion.2), channel_id=1, source_target_pairs={{1,2},{2,1},{5,6},{6,5},{9,10},{10,9},{13,14},{14,13},{17,18},{18,... | collective-permute-start | bytes 3145736 | tf_op jit(solution)/shard_map/ppermute | solution.py:308
  24.3 17.7 %collective-permute-start.5 = (bf16[256,1024]{0,1:T(8,128)(2,1)}, bf16[256,1024]{0,1:T(8,128)(2,1)S(1)}, u32[]{:S(2)}, u32[]{:S(2)}) collective-permute-start(bf16[256,1024]{0,1:T(8,128)(2,1)} %get-tuple-element.54), channel_id=1, source_target_pairs={{16,0},{20,8},{24,16},{28,24},{17,1},{21,9},{25,17},{29,25},{2,2},... | collective-permute-start | bytes 1572872 | tf_op jit(solution)/shard_map/ppermute | solution.py:299
  25.6 16.5 %collective-permute-start.6 = (bf16[256,1024]{0,1:T(8,128)(2,1)S(1)}, bf16[256,1024]{0,1:T(8,128)(2,1)}, u32[]{:S(2)}, u32[]{:S(2)}) collective-permute-start(bf16[256,1024]{0,1:T(8,128)(2,1)S(1)} %get-tuple-element.53), channel_id=1, source_target_pairs={{16,4},{20,12},{24,20},{28,28},{17,5},{21,13},{25,21},{29,29},{2,6... | collective-permute-start | bytes 1572872 | tf_op jit(solution)/shard_map/ppermute | solution.py:300
  41.7 110.9 %copy-start = (bf16[8192,128]{1,0:T(8,128)(2,1)}, bf16[8192,128]{1,0:T(8,128)(2,1)S(1)}, u32[]{:S(2)}) copy-start(bf16[8192,128]{1,0:T(8,128)(2,1)S(1)} %fusion.refs_12_.refs_22_) | copy-start | bytes 6291460
  42.1 44.4 %collective-permute-start.7 = (bf16[1024,256]{1,0:T(8,128)(2,1)S(1)}, bf16[1024,256]{1,0:T(8,128)(2,1)S(1)}, u32[]{:S(2)}, u32[]{:S(2)}) collective-permute-start(bf16[1024,256]{1,0:T(8,128)(2,1)S(1)} %select_bitcast_fusion), channel_id=1, source_target_pairs={{0,1},{3,2},{4,5},{7,6},{8,9},{11,10},{12,13},{15,14},{16,17},{19,... | collective-permute-start | bytes 1572872 | tf_op jit(solution)/shard_map/ppermute | solution.py:308
  86.5 0.8 copy-start.6
  90.4 2.1 copy-start.9
  93.4 46.5 %collective-permute-start.3 = (bf16[1024,512]{1,0:T(8,128)(2,1)}, bf16[1024,512]{1,0:T(8,128)(2,1)}, u32[]{:S(2)}, u32[]{:S(2)}) collective-permute-start(bf16[1024,512]{1,0:T(8,128)(2,1)} %pad_maximum_fusion.2), channel_id=1, source_target_pairs={{0,1},{1,0},{2,3},{3,2},{4,5},{5,4},{6,7},{7,6},{8,9},{9,8},{10,11... | collective-permute-start | bytes 3145736 | tf_op jit(solution)/shard_map/ppermute | solution.py:308
  99.0 53.7 %collective-permute-start.8 = (bf16[512,1024]{1,0:T(8,128)(2,1)}, bf16[512,1024]{1,0:T(8,128)(2,1)}, u32[]{:S(2)}, u32[]{:S(2)}) collective-permute-start(bf16[512,1024]{1,0:T(8,128)(2,1)} %get-tuple-element.29), channel_id=1, source_target_pairs={{0,1},{3,2},{4,5},{7,6},{8,9},{11,10},{12,13},{15,14},{16,17},{19,... | collective-permute-start | bytes 3145736 | tf_op jit(solution)/shard_map/ppermute | solution.py:308
  104.2 48.4 %collective-permute-start.4 = (bf16[1024,512]{1,0:T(8,128)(2,1)}, bf16[1024,512]{1,0:T(8,128)(2,1)}, u32[]{:S(2)}, u32[]{:S(2)}) collective-permute-start(bf16[1024,512]{1,0:T(8,128)(2,1)} %pad_maximum_fusion.3), channel_id=1, source_target_pairs={{1,2},{2,1},{5,6},{6,5},{9,10},{10,9},{13,14},{14,13},{17,18},{18,... | collective-permute-start | bytes 3145736 | tf_op jit(solution)/shard_map/ppermute | solution.py:308
  105.8 71.2 %collective-permute-start.10 = (bf16[768,1024]{1,0:T(8,128)(2,1)}, bf16[768,1024]{1,0:T(8,128)(2,1)}, u32[]{:S(2)}, u32[]{:S(2)}) collective-permute-start(bf16[768,1024]{1,0:T(8,128)(2,1)} %fusion.2), channel_id=1, source_target_pairs={{0,1},{3,2},{4,5},{7,6},{8,9},{11,10},{12,13},{15,14},{16,17},{19,... | collective-permute-start | bytes 4718600 | tf_op jit(solution)/shard_map/ppermute | solution.py:308
  112.0 65.0 %collective-permute-start.9 = (bf16[1024,768]{1,0:T(8,128)(2,1)}, bf16[1024,768]{1,0:T(8,128)(2,1)}, u32[]{:S(2)}, u32[]{:S(2)}) collective-permute-start(bf16[1024,768]{1,0:T(8,128)(2,1)} %pad_maximum_fusion.1), channel_id=1, source_target_pairs={{1,2},{2,1},{5,6},{6,5},{9,10},{10,9},{13,14},{14,13},{17,18},{18,... | collective-permute-start | bytes 4718600 | tf_op jit(solution)/shard_map/ppermute | solution.py:308
  113.9 1.0 copy-start.1
  152.7 1.0 copy-start.2
  153.7 23.3 %copy-start.5 = (bf16[512,1024]{1,0:T(8,128)(2,1)S(1)}, bf16[512,1024]{1,0:T(8,128)(2,1)}, u32[]{:S(2)}) copy-start(bf16[512,1024]{1,0:T(8,128)(2,1)} %get-tuple-element.35) | copy-start | bytes 3145732
  177.0 25.1 %copy-start.3 = (f32[16,8192]{1,0:T(8,128)S(1)}, f32[16,8192]{1,0:T(8,128)}, u32[]{:S(2)}) copy-start(f32[16,8192]{1,0:T(8,128)} %subtract_convert_fusion.1.refs_11_.refs_21_) | copy-start | bytes 1572868
  177.0 25.1 %collective-permute-start.12 = (bf16[512,1024]{1,0:T(8,128)(2,1)S(1)}, bf16[512,1024]{1,0:T(8,128)(2,1)S(1)}, u32[]{:S(2)}, u32[]{:S(2)}) collective-permute-start(bf16[512,1024]{1,0:T(8,128)(2,1)S(1)} %copy-done.5), channel_id=1, source_target_pairs={{0,1},{3,2},{4,5},{7,6},{8,9},{11,10},{12,13},{15,14},{16,17},{19,... | collective-permute-start | bytes 3145736 | tf_op jit(solution)/shard_map/ppermute | solution.py:308
  181.6 20.5 %collective-permute-start.11 = (bf16[1024,512]{1,0:T(8,128)(2,1)}, bf16[1024,512]{1,0:T(8,128)(2,1)S(1)}, u32[]{:S(2)}, u32[]{:S(2)}) collective-permute-start(bf16[1024,512]{1,0:T(8,128)(2,1)} %collective-permute-done.3.refs_2_.refs_3_), channel_id=1, source_target_pairs={{1,2},{2,1},{5,6},{6,5},{9,10},{10,9},{13,14},{14,13},{17,18},{18,... | collective-permute-start | bytes 3145736 | tf_op jit(solution)/shard_map/ppermute | solution.py:308
  206.9 1.3 collective-permute-start.13
  208.3 4.3 %collective-permute-start.14 = (f32[2,8192]{1,0:T(2,128)S(1)}, f32[2,8192]{1,0:T(2,128)S(1)}, u32[]{:S(2)}, u32[]{:S(2)}) collective-permute-start(f32[2,8192]{1,0:T(2,128)S(1)} %fusion.42), channel_id=1, source_target_pairs={{0,8},{4,12},{8,0},{12,4},{16,24},{20,28},{24,16},{28,20},{1,9},{5... | collective-permute-start | bytes 196616 | tf_op jit(solution)/shard_map/ppermute | solution.py:223
  212.8 4.3 %collective-permute-start.15 = (f32[2,8192]{1,0:T(2,128)S(1)}, f32[2,8192]{1,0:T(2,128)S(1)}, u32[]{:S(2)}, u32[]{:S(2)}) collective-permute-start(f32[2,8192]{1,0:T(2,128)S(1)} %fusion.43), channel_id=1, source_target_pairs={{0,16},{4,20},{8,24},{12,28},{16,0},{20,4},{24,8},{28,12},{1,17},{... | collective-permute-start | bytes 196616 | tf_op jit(solution)/shard_map/ppermute | solution.py:223
  217.1 26.8 %collective-permute-start.16 = (f32[2,8192]{1,0:T(2,128)S(1)}, f32[2,8192]{1,0:T(2,128)S(1)}, u32[]{:S(2)}, u32[]{:S(2)}) collective-permute-start(f32[2,8192]{1,0:T(2,128)S(1)} %add.136), channel_id=1, source_target_pairs={{0,1},{1,0},{2,3},{3,2},{4,5},{5,4},{6,7},{7,6},{8,9},{9,8},{10,11... | collective-permute-start | bytes 196616 | tf_op jit(solution)/shard_map/ppermute | solution.py:223
  243.9 5.2 %collective-permute-start.17 = (f32[2,8192]{1,0:T(2,128)S(1)}, f32[2,8192]{1,0:T(2,128)S(1)}, u32[]{:S(2)}, u32[]{:S(2)}) collective-permute-start(f32[2,8192]{1,0:T(2,128)S(1)} %add.137), channel_id=1, source_target_pairs={{0,2},{1,3},{2,0},{3,1},{4,6},{5,7},{6,4},{7,5},{8,10},{9,11},{10,... | collective-permute-start | bytes 196616 | tf_op jit(solution)/shard_map/ppermute | solution.py:223
Sparse Core Ops, SparseCore 0:
  9.2 66.4 all-gather.2
  87.5 36.8 all-gather.4
